TPU v7x, 128 devices: a whole 4x4x4 slice. The times are simulated.
128 devices in a mesh: ctx: 16 (over y_lo, z, core), head: 8 (over y_hi, x).
Axes of the slice: x: 4, y: 4 (y_hi: 2, y_lo: 2; y = y_hi * 2 + y_lo), z: 4, core: 2. Of those that a mesh axis runs over, the one named last changes fastest.
Arguments:
- queries: bfloat16 [64, 2, 8192], P('ctx', None, 'head'), may hold values from -16 to 16
- prefix_k: bfloat16 [262144, 1024], P('ctx', 'head'), may hold values from -10 to 10
- prefix_v: bfloat16 [262144, 1024], P('ctx', 'head'), may hold values from -7 to 7
- suffix_k: bfloat16 [96, 4096, 1024], P('ctx', None, 'head'), may hold values from -6 to 6
- suffix_v: bfloat16 [96, 4096, 1024], P('ctx', None, 'head'), may hold values from -6 to 6
- new_k: bfloat16 [64, 2, 1024], P('ctx', None, 'head'), may hold values from -10 to 10
- new_v: bfloat16 [64, 2, 1024], P('ctx', None, 'head'), may hold values from -6 to 6
- suffix_len: int32 [64], replicated, may hold values from 1 to 4096, 131072 in all
- owner_of: int32 [64], replicated, may hold values from 0 to 95, as said below
Outputs:
- attended: bfloat16 [64, 2, 8192], P('ctx')
Inputs may be any that keep to these rules, and one draw needn't show every extreme that they name: `owner_of`: every request names a different slot; slot g belongs to ctx index g // 6; in every draw all 6 slots of some owner are taken.
All inputs are finite; a program needn't handle non-finite values.
Results may differ from a plain program's by a relative error of at most 0.0054.
Values may be sent and summed in bfloat16 or wider, within the bound.
No kernel may reach another device: no remote copies, remote signals or barrier semaphores. Data moves between devices by JAX's collectives and lax.ppermute only.
A program may use at most 64 MiB of HBM per device.

v0:
```python
import functools

import jax
import jax.numpy as jnp
from jax import lax
from jax.experimental import pallas as pl
from jax.experimental.pallas import tpu as pltpu
from jax.sharding import PartitionSpec as P

H = 64
KV = 8
HD = 128
LOG2E = 1.4426950408889634
NEG_BIG = -1e30
SAFE_SUM = 2.0**60

CHUNK = 4096
TILE = 256

f32 = jnp.float32
bf16 = jnp.bfloat16


def dot(a, b):
    return lax.dot_general(a, b, (((1,), (0,)), ((), ())), preferred_element_type=f32)


def dot_t(a, b):
    return lax.dot_general(a, b, (((1,), (1,)), ((), ())), preferred_element_type=f32)


def lane_sum(x):
    return jnp.broadcast_to(jnp.sum(x, axis=1, keepdims=True), x.shape)


def pieces(x):
    first = x.astype(bf16)
    rest = x - first.astype(f32)
    second = rest.astype(bf16)
    third = (rest - second.astype(f32)).astype(bf16)
    return first, second, third


def spread_kernel(copies, q_ref, k_ref, v_ref, out_ref):
    rows = q_ref.shape[0] * q_ref.shape[1]
    width = q_ref.shape[2]
    block = jnp.concatenate(
        [
            q_ref[...].astype(f32).reshape(rows, width),
            k_ref[...].astype(f32).reshape(rows, HD),
            v_ref[...].astype(f32).reshape(rows, HD),
        ],
        axis=1,
    )
    out_ref[...] = jnp.concatenate([block] * copies, axis=0).astype(bf16)


def attend_kernel(
    scale, slots_ref, q_ref, pk_ref, pv_ref, sk_ref, sv_ref, out_ref,
    kbuf, vbuf, skbuf, svbuf, qrow, top, acc, total, qslot, oslot, lslot, ksem, vsem, ssem,
):
    req_rows = q_ref.shape[0]
    groups = (q_ref.shape[1] - 2 * HD) // HD
    rows = req_rows * groups
    slot_count, span = sk_ref.shape[0], sk_ref.shape[1]
    chunks = pk_ref.shape[0] // CHUNK

    def prefix_copies(i):
        at = pl.ds(i * CHUNK, CHUNK)
        return (
            pltpu.make_async_copy(pk_ref.at[at], kbuf.at[at], ksem.at[i]),
            pltpu.make_async_copy(pv_ref.at[at], vbuf.at[at], vsem.at[i]),
        )

    def suffix_copies(s):
        return (
            pltpu.make_async_copy(sk_ref.at[s], skbuf.at[s], ssem.at[0, s]),
            pltpu.make_async_copy(sv_ref.at[s], svbuf.at[s], ssem.at[1, s]),
        )

    for i in range(chunks):
        for copy in prefix_copies(i):
            copy.start()
    for s in range(slot_count):
        for copy in suffix_copies(s):
            copy.start()

    for g in range(groups):
        qrow[g * req_rows : (g + 1) * req_rows] = q_ref[:, g * HD : (g + 1) * HD]
    acc[...] = jnp.zeros_like(acc)
    total[...] = jnp.zeros_like(total)

    def chunk_step(i, unused):
        for copy in prefix_copies(i):
            copy.wait()

        @pl.when(i == 0)
        def _():
            for r in range(0, rows, TILE):
                s = dot_t(qrow[r : r + TILE], kbuf[0:TILE]) * scale
                top[r : r + TILE] = jnp.broadcast_to(jnp.max(s, axis=1, keepdims=True), (TILE, HD))

        shift = jnp.concatenate([top[...]] * (TILE // HD), axis=1)
        mix = None
        weight_sum = None
        for t in range(0, CHUNK, TILE):
            at = pl.ds(pl.multiple_of(i * CHUNK + t, TILE), TILE)
            p = jnp.exp2(dot_t(qrow[...], kbuf[at]) * scale - shift)
            part = dot(p.astype(bf16), vbuf[at])
            part_sum = sum(p[:, u : u + HD] for u in range(0, TILE, HD))
            mix = part if mix is None else mix + part
            weight_sum = part_sum if weight_sum is None else weight_sum + part_sum
        acc[...] += mix
        total[...] += weight_sum
        return 0

    lax.fori_loop(0, chunks, chunk_step, 0)
    total[...] = lane_sum(total[...])

    @pl.when(jnp.logical_not(jnp.max(total[...]) < SAFE_SUM))
    def _():
        def safe_rows(j, unused):
            at = pl.ds(pl.multiple_of(j * TILE, TILE), TILE)
            q = qrow[at]

            def safe_keys(i, carried):
                high, summed, mixed = carried
                keys = pl.ds(pl.multiple_of(i * TILE, TILE), TILE)
                s = dot_t(q, kbuf[keys]) * scale
                new = jnp.maximum(high, jnp.broadcast_to(jnp.max(s, axis=1, keepdims=True), high.shape))
                p = jnp.exp2(s - jnp.concatenate([new] * (TILE // HD), axis=1))
                decay = jnp.exp2(high - new)
                part = jnp.broadcast_to(jnp.sum(p, axis=1, keepdims=True), high.shape)
                return new, summed * decay + part, mixed * decay + dot(p.astype(bf16), vbuf[keys])

            zero = jnp.zeros((TILE, HD), f32)
            high, summed, mixed = lax.fori_loop(
                0, chunks * CHUNK // TILE, safe_keys, (zero + NEG_BIG, zero, zero)
            )
            top[at] = high
            total[at] = summed
            acc[at] = mixed
            return 0

        lax.fori_loop(0, rows // TILE, safe_rows, 0)

    tokens = 2
    pad = 16
    pick_row = lax.broadcasted_iota(jnp.int32, (pad, req_rows), 0)
    pick_col = lax.broadcasted_iota(jnp.int32, (pad, req_rows), 1)
    put_row = lax.broadcasted_iota(jnp.int32, (req_rows, pad), 0)
    put_col = lax.broadcasted_iota(jnp.int32, (req_rows, pad), 1)
    pick_at = jnp.full((pad, req_rows), -1, jnp.int32)
    put_at = jnp.full((req_rows, pad), -1, jnp.int32)
    for s in range(slot_count):
        row = slots_ref[s] * tokens
        pick_at = jnp.where(pick_row // tokens == s, row + pick_row % tokens, pick_at)
        put_at = jnp.where(put_col // tokens == s, row + put_col % tokens, put_at)
    pick = jnp.where(pick_at == pick_col, 1.0, 0.0).astype(bf16)
    put_f = jnp.where(put_at == put_row, 1.0, 0.0)
    put = put_f.astype(bf16)
    picked = dot(pick, q_ref[...])
    new_keys = picked[:, groups * HD : (groups + 1) * HD].astype(bf16)
    new_values = picked[:, (groups + 1) * HD :].astype(bf16)
    slot_rows = groups * tokens
    for s in range(slot_count):
        for g in range(groups):
            qslot[s * slot_rows + g * tokens : s * slot_rows + (g + 1) * tokens] = picked[
                s * tokens : (s + 1) * tokens, g * HD : (g + 1) * HD
            ]
    oslot[...] = jnp.zeros_like(oslot)
    lslot[...] = jnp.zeros_like(lslot)
    fresh_row = lax.broadcasted_iota(jnp.int32, (slot_rows, pad), 0)
    fresh_col = lax.broadcasted_iota(jnp.int32, (slot_rows, pad), 1)
    position = lax.broadcasted_iota(jnp.int32, (slot_rows, span), 1)
    for s in range(slot_count):
        for copy in suffix_copies(s):
            copy.wait()
    for s in range(slot_count):
        q = qslot[s * slot_rows : (s + 1) * slot_rows].astype(bf16)
        live = position < slots_ref[slot_count + s]
        causal = (fresh_col // tokens == s) & (fresh_col % tokens <= fresh_row % tokens)
        scores = jnp.where(live, dot_t(q, skbuf[s]) * scale, NEG_BIG)
        fresh = jnp.where(causal, dot_t(q, new_keys) * scale, NEG_BIG)
        high = jnp.maximum(jnp.max(scores, axis=1, keepdims=True), jnp.max(fresh, axis=1, keepdims=True))
        p = jnp.exp2(scores - high)
        fresh_p = jnp.exp2(fresh - high)
        summed = jnp.sum(p, axis=1, keepdims=True) + jnp.sum(fresh_p, axis=1, keepdims=True)
        mixed = dot(p.astype(bf16), svbuf[s]) + dot(fresh_p.astype(bf16), new_values)
        mixed = mixed / summed
        level = jnp.broadcast_to(high + jnp.log(summed) * LOG2E, mixed.shape)
        for g in range(groups):
            put_at_rows = slice(s * tokens, (s + 1) * tokens)
            lanes = slice(g * HD, (g + 1) * HD)
            oslot[put_at_rows, lanes] = mixed[g * tokens : (g + 1) * tokens]
            lslot[put_at_rows, lanes] = level[g * tokens : (g + 1) * tokens]

    suffix_mix = sum(dot(put, piece) for piece in pieces(oslot[...]))
    suffix_level = sum(dot(put, piece) for piece in pieces(lslot[...]))
    has_suffix = jnp.sum(put_f, axis=1, keepdims=True) > 0.5
    lane = lax.broadcasted_iota(jnp.int32, (req_rows, HD), 1)
    levels = jnp.zeros((req_rows, HD), f32)
    for g in range(groups):
        at = slice(g * req_rows, (g + 1) * req_rows)
        lanes = slice(g * HD, (g + 1) * HD)
        level = top[at] + jnp.log(total[at]) * LOG2E
        other = jnp.where(has_suffix, suffix_level[:, lanes], NEG_BIG)
        high = jnp.maximum(level, other)
        mine = jnp.exp2(level - high)
        theirs = jnp.exp2(other - high)
        summed = mine + theirs
        mixed = (acc[at] / total[at] * mine + suffix_mix[:, lanes] * theirs) / summed
        out_ref[:, lanes] = mixed.astype(bf16)
        level = high + jnp.log(summed) * LOG2E
        for j, piece in enumerate(pieces(level)):
            levels = jnp.where(lane == j * groups + g, piece.astype(f32), levels)
    out_ref[:, groups * HD :] = levels.astype(bf16)


def merge_kernel(sources, copies, part_ref, out_ref):
    rows = part_ref.shape[0]
    home_rows = rows // sources
    groups = (part_ref.shape[1] - HD) // HD
    levels = part_ref[:, groups * HD :].astype(f32)
    lane = lax.broadcasted_iota(jnp.int32, (rows, HD), 1)
    for g in range(groups):
        mine = (lane % groups == g) & (lane < 3 * groups)
        level = lane_sum(jnp.where(mine, levels, 0.0)).reshape(sources, home_rows, HD)
        weight = jnp.exp2(level - jnp.max(level, axis=0, keepdims=True))
        part = part_ref[:, g * HD : (g + 1) * HD].astype(f32).reshape(sources, home_rows, HD)
        mixed = jnp.sum(part * weight, axis=0) / jnp.sum(weight, axis=0)
        out_ref[:, g * HD : (g + 1) * HD] = jnp.concatenate([mixed] * copies, axis=0).astype(bf16)


def on_device(queries, prefix_k, prefix_v, suffix_k, suffix_v, new_k, new_v, suffix_len, owner_of):
    req_local, tokens, width = queries.shape
    groups = width // HD
    slot_count, span = suffix_k.shape[0], suffix_k.shape[1]
    ctx_count = lax.axis_size("ctx")
    head_count = lax.axis_size("head")
    ctx_index = lax.axis_index("ctx")
    home_rows = req_local * tokens
    all_rows = ctx_count * home_rows
    rows = all_rows * groups
    vmem = pl.BlockSpec(memory_space=pltpu.VMEM)
    smem = pl.BlockSpec(memory_space=pltpu.SMEM)
    hbm = pl.BlockSpec(memory_space=pl.ANY)

    sent = pl.pallas_call(
        functools.partial(spread_kernel, ctx_count),
        in_specs=[vmem] * 3,
        out_specs=vmem,
        out_shape=jax.ShapeDtypeStruct((all_rows, width + 2 * HD), bf16),
        name="spread",
    )(queries, new_k, new_v)
    gathered = lax.all_to_all(sent, "ctx", split_axis=0, concat_axis=0, tiled=True)

    my_slots = ctx_index * slot_count + jnp.arange(slot_count, dtype=jnp.int32)
    incoming = owner_of[None, :] == my_slots[:, None]
    request = jnp.arange(owner_of.shape[0], dtype=jnp.int32)
    slot_request = jnp.max(jnp.where(incoming, request[None, :], -4), axis=1)
    slot_length = jnp.sum(jnp.where(incoming, suffix_len[None, :], 0), axis=1)
    slots = jnp.concatenate([slot_request, slot_length])

    chunks = prefix_k.shape[0] // CHUNK
    parts = pl.pallas_call(
        functools.partial(attend_kernel, HD**-0.5 * LOG2E),
        in_specs=[smem, vmem, hbm, hbm, hbm, hbm],
        out_specs=vmem,
        out_shape=jax.ShapeDtypeStruct((all_rows, width + HD), bf16),
        scratch_shapes=[
            pltpu.VMEM(prefix_k.shape, bf16),
            pltpu.VMEM(prefix_v.shape, bf16),
            pltpu.VMEM(suffix_k.shape, bf16),
            pltpu.VMEM(suffix_v.shape, bf16),
            pltpu.VMEM((rows, HD), bf16),
            pltpu.VMEM((rows, HD), f32),
            pltpu.VMEM((rows, HD), f32),
            pltpu.VMEM((rows, HD), f32),
            pltpu.VMEM((slot_count * groups * tokens, HD), f32),
            pltpu.VMEM((16, width), f32),
            pltpu.VMEM((16, width), f32),
            pltpu.SemaphoreType.DMA((chunks,)),
            pltpu.SemaphoreType.DMA((chunks,)),
            pltpu.SemaphoreType.DMA((2, slot_count)),
        ],
        compiler_params=pltpu.CompilerParams(vmem_limit_bytes=56 * 1024 * 1024),
        name="attend",
    )(slots, gathered, prefix_k, prefix_v, suffix_k, suffix_v)
    arrived = lax.all_to_all(parts, "ctx", split_axis=0, concat_axis=0, tiled=True)

    finished = pl.pallas_call(
        functools.partial(merge_kernel, ctx_count, head_count),
        in_specs=[vmem],
        out_specs=vmem,
        out_shape=jax.ShapeDtypeStruct((head_count * home_rows, width), bf16),
        name="merge",
    )(arrived)
    heads = lax.all_to_all(finished, "head", split_axis=0, concat_axis=0, tiled=True)
    heads = heads.reshape(head_count, home_rows, width).transpose(1, 0, 2)
    return heads.reshape(req_local, tokens, head_count * width)


def solution(mesh):
    placed = (
        P("ctx", None, "head"),
        P("ctx", "head"),
        P("ctx", "head"),
        P("ctx", None, "head"),
        P("ctx", None, "head"),
        P("ctx", None, "head"),
        P("ctx", None, "head"),
        P(),
        P(),
    )
    return jax.shard_map(
        on_device, mesh=mesh, in_specs=placed, out_specs=P("ctx", None, None), check_vma=False
    )
```

profile of v0, /device:TPU:0, one launch (start us, length us, event | category | flops | bytes accessed | tf_op | source)
XLA Modules:
  0.0 187.9 jit_solution(62230494151054311)
XLA Ops:
  0.0 1.5 spread.1
  1.5 6.5 %all-to-all-start = ((bf16[16,8,1280]{2,1,0:T(8,128)(2,1)}), bf16[16,8,1280]{2,1,0:T(8,128)(2,1)S(1)}, u32[]{:S(2)}, u32[]{:S(2)}) async-start(bf16[16,8,1280]{2,1,0:T(8,128)(2,1)} %bitcast.6), calls=%async_computation | async-start | bytes 655360 | tf_op jit(solution)/shard_map/all_to_all | solution.py:256
  8.0 0.9 fusion
  8.9 0.6 pad_add_fusion.slots_ref
  9.5 7.3 %all-to-all-done = bf16[16,8,1280]{2,1,0:T(8,128)(2,1)S(1)} async-done(((bf16[16,8,1280]{2,1,0:T(8,128)(2,1)}), bf16[16,8,1280]{2,1,0:T(8,128)(2,1)S(1)}, u32[]{:S(2)}, u32[]{:S(2)}) %all-to-all-start) | async-done | bytes 327712 | tf_op jit(solution)/shard_map/all_to_all | solution.py:256
  16.7 0.0 copy-start
  16.8 0.7 copy-done
  17.5 30.5 %attend.1 = bf16[128,1152]{1,0:T(8,128)(2,1)} custom-call(s32[12]{0:T(128)} %pad_add_fusion.slots_ref, bf16[128,1280]{1,0:T(8,128)(2,1)} %bitcast.7, bf16[16384,128]{1,0:T(8,128)(2,1)} %pk_ref.1, bf16[16384,128]{1,0:T(8,128)(2,1)} %pv_ref.1, bf16[6,4096,128]{2,1,0:T(8,128)(2,1)} %sk_ref.1, bf16[6,4096,128]{2,1,0:T(8,128)(2,1)} %sv_ref.1), custom_call_target="tpu_custom_call" | custom-call | tf_op jit(solution)/shard_map/attend/pallas_call | solution.py:266
  48.0 122.4 %all_to_all.31 = bf16[16,8,1152]{2,1,0:T(8,128)(2,1)} all-to-all(bf16[16,8,1152]{2,1,0:T(8,128)(2,1)} %bitcast.9), channel_id=1, replica_groups=mesh['ctx'=16,'head'=8] {'ctx'}, dimensions={0} | all-to-all | bytes 589824 | tf_op jit(solution)/shard_map/all_to_all | solution.py:290
  170.4 1.9 %merge.1 = bf16[64,1024]{1,0:T(8,128)(2,1)} custom-call(bf16[128,1152]{1,0:T(8,128)(2,1)} %bitcast.8), custom_call_target="tpu_custom_call" | custom-call | tf_op jit(solution)/shard_map/merge/pallas_call | solution.py:292
  172.3 14.7 %all_to_all.32 = bf16[8,8,1024]{2,1,0:T(8,128)(2,1)S(1)} all-to-all(bf16[8,8,1024]{2,1,0:T(8,128)(2,1)} %bitcast.10), channel_id=1, replica_groups=mesh['ctx'=16,'head'=8] {'head'}, dimensions={0} | all-to-all | bytes 262144 | tf_op jit(solution)/shard_map/all_to_all | solution.py:299
  187.1 0.1 copy.11
  187.1 0.7 reshape.17
  (1 shorter events, 0.0 us)
Async XLA Ops:
  1.5 15.3 %all-to-all-start = ((bf16[16,8,1280]{2,1,0:T(8,128)(2,1)}), bf16[16,8,1280]{2,1,0:T(8,128)(2,1)S(1)}, u32[]{:S(2)}, u32[]{:S(2)}) async-start(bf16[16,8,1280]{2,1,0:T(8,128)(2,1)} %bitcast.6), calls=%async_computation | async-start | bytes 655360 | tf_op jit(solution)/shard_map/all_to_all | solution.py:256
  16.7 0.7 copy-start
where the time goes:
time: 189 us; the launch traced here: 188 us
  blocking collectives  137 us (72%)
  Pallas kernels  33.9 us (18%)
  waiting for transfers between devices  7.26 us (4%)
  starting transfers between devices  6.51 us (3%)
    all_to_all x1, blocking collectives, on_device(): lax.all_to_all(parts, 'ctx', split_axis=0, concat_axis=0, tiled=True)  122 us
    pallas_call x1, Pallas kernels, on_device(): pl.pallas_call(functools.partial(attend_kernel, HD ** (-0.5) * LOG2E), in...  30.5 us
    all_to_all x1, blocking collectives, on_device(): lax.all_to_all(finished, 'head', split_axis=0, concat_axis=0, tiled=True)  14.7 us
    all_to_all x1, waiting for transfers between devices, on_device(): lax.all_to_all(sent, 'ctx', split_axis=0, concat_axis=0, tiled=True)  7.26 us
    all_to_all x1, starting transfers between devices, on_device(): lax.all_to_all(sent, 'ctx', split_axis=0, concat_axis=0, tiled=True)  6.51 us
  transfers between devices with their start and end apart: 1, of which 1 were waited for; matrix products, arithmetic and copies ran while one was open for 1% of the time, Pallas kernels for 0%

commit v1 on v0

--- a/solution.py
+++ b/solution.py
@@ -14,8 +14,11 @@
 NEG_BIG = -1e30
 SAFE_SUM = 2.0**60
 
+TOKENS = 2
+PAD = 16
 CHUNK = 4096
 TILE = 256
+SUFFIX_AT = (1, 5, 9)
 
 f32 = jnp.float32
 bf16 = jnp.bfloat16
@@ -57,13 +60,15 @@
 
 def attend_kernel(
     scale, slots_ref, q_ref, pk_ref, pv_ref, sk_ref, sv_ref, out_ref,
-    kbuf, vbuf, skbuf, svbuf, qrow, top, acc, total, qslot, oslot, lslot, ksem, vsem, ssem,
+    kbuf, vbuf, skbuf, svbuf, qrow, top, acc, total, qslot, oraw, lraw, oslot, lslot, ksem, vsem, ssem,
 ):
     req_rows = q_ref.shape[0]
     groups = (q_ref.shape[1] - 2 * HD) // HD
     rows = req_rows * groups
     slot_count, span = sk_ref.shape[0], sk_ref.shape[1]
+    slot_rows = groups * TOKENS
     chunks = pk_ref.shape[0] // CHUNK
+    per_step = slot_count // (chunks - 1)
 
     def prefix_copies(i):
         at = pl.ds(i * CHUNK, CHUNK)
@@ -78,43 +83,131 @@
             pltpu.make_async_copy(sv_ref.at[s], svbuf.at[s], ssem.at[1, s]),
         )
 
-    for i in range(chunks):
-        for copy in prefix_copies(i):
-            copy.start()
-    for s in range(slot_count):
-        for copy in suffix_copies(s):
-            copy.start()
+    for copy in prefix_copies(0):
+        copy.start()
 
     for g in range(groups):
         qrow[g * req_rows : (g + 1) * req_rows] = q_ref[:, g * HD : (g + 1) * HD]
     acc[...] = jnp.zeros_like(acc)
     total[...] = jnp.zeros_like(total)
 
-    def chunk_step(i, unused):
+    pick_row = lax.broadcasted_iota(jnp.int32, (PAD, req_rows), 0)
+    pick_col = lax.broadcasted_iota(jnp.int32, (PAD, req_rows), 1)
+    put_row = lax.broadcasted_iota(jnp.int32, (req_rows, PAD), 0)
+    put_col = lax.broadcasted_iota(jnp.int32, (req_rows, PAD), 1)
+    pick_at = jnp.full((PAD, req_rows), -1, jnp.int32)
+    put_at = jnp.full((req_rows, PAD), -1, jnp.int32)
+    for s in range(slot_count):
+        row = slots_ref[s] * TOKENS
+        pick_at = jnp.where(pick_row // TOKENS == s, row + pick_row % TOKENS, pick_at)
+        put_at = jnp.where(put_col // TOKENS == s, row + put_col % TOKENS, put_at)
+    pick = jnp.where(pick_at == pick_col, 1.0, 0.0).astype(bf16)
+    picked = dot(pick, q_ref[...])
+    new_keys = picked[:, groups * HD : (groups + 1) * HD].astype(bf16)
+    new_values = picked[:, (groups + 1) * HD :].astype(bf16)
+    for s in range(slot_count):
+        for g in range(groups):
+            qslot[s * slot_rows + g * TOKENS : s * slot_rows + (g + 1) * TOKENS] = picked[
+                s * TOKENS : (s + 1) * TOKENS, g * HD : (g + 1) * HD
+            ]
+    fresh_row = lax.broadcasted_iota(jnp.int32, (slot_rows, PAD), 0)
+    fresh_col = lax.broadcasted_iota(jnp.int32, (slot_rows, PAD), 1)
+    position = lax.broadcasted_iota(jnp.int32, (slot_rows, span), 1)
+
+    def suffix_stages(slots):
+        held = {}
+        count = len(slots)
+
+        def blocks(make):
+            return jnp.concatenate([make(s) for s in slots], axis=0)
+
+        def apart(x):
+            zero = jnp.zeros((slot_rows, HD), x.dtype)
+            own = [x[n * slot_rows : (n + 1) * slot_rows] for n in range(count)]
+            return jnp.concatenate(
+                [jnp.concatenate([own[n] if m == n else zero for m in range(count)], axis=1) for n in range(count)],
+                axis=0,
+            )
+
+        def score():
+            q = blocks(lambda s: qslot[pl.ds(pl.multiple_of(s * slot_rows, slot_rows), slot_rows)])
+            causal = blocks(
+                lambda s: (fresh_col // TOKENS == s) & (fresh_col % TOKENS <= fresh_row % TOKENS)
+            )
+            live = blocks(lambda s: position < slots_ref[slot_count + s])
+            keys = jnp.concatenate([skbuf[s] for s in slots], axis=1)
+            held["scores"] = jnp.where(live, dot_t(apart(q).astype(bf16), keys) * scale, NEG_BIG)
+            held["fresh"] = jnp.where(causal, dot_t(q.astype(bf16), new_keys) * scale, NEG_BIG)
+
+        def weigh():
+            scores, fresh = held["scores"], held["fresh"]
+            high = jnp.maximum(
+                jnp.max(scores, axis=1, keepdims=True), jnp.max(fresh, axis=1, keepdims=True)
+            )
+            p = jnp.exp2(scores - high)
+            fresh_p = jnp.exp2(fresh - high)
+            held["sum"] = jnp.sum(p, axis=1, keepdims=True) + jnp.sum(fresh_p, axis=1, keepdims=True)
+            held["high"], held["p"], held["fresh_p"] = high, p.astype(bf16), fresh_p.astype(bf16)
+
+        def mix():
+            values = jnp.concatenate([svbuf[s] for s in slots], axis=1)
+            wide = dot(held["p"], values)
+            fresh_mix = dot(held["fresh_p"], new_values)
+            level = held["high"] + jnp.log(held["sum"]) * LOG2E
+            for n, s in enumerate(slots):
+                at = slice(n * slot_rows, (n + 1) * slot_rows)
+                mixed = wide[at, n * HD : (n + 1) * HD] + fresh_mix[at]
+                oraw[s] = mixed / held["sum"][at]
+                lraw[s] = jnp.broadcast_to(level[at], mixed.shape)
+
+        return [score, weigh, mix]
+
+    def chunk_step(i, slots):
+        stages = {}
         for copy in prefix_copies(i):
             copy.wait()
-
-        @pl.when(i == 0)
-        def _():
+        if slots:
+            for s in slots:
+                for copy in suffix_copies(s):
+                    copy.wait()
+            stages = dict(zip(SUFFIX_AT, suffix_stages(slots)))
+
+        def start_next():
+            for copy in prefix_copies(i + 1):
+                copy.start()
+            for n in range(per_step):
+                for copy in suffix_copies(i * per_step + n):
+                    copy.start()
+
+        if slots:
+            pl.when(i + 1 < chunks)(start_next)
+        else:
+            start_next()
             for r in range(0, rows, TILE):
                 s = dot_t(qrow[r : r + TILE], kbuf[0:TILE]) * scale
                 top[r : r + TILE] = jnp.broadcast_to(jnp.max(s, axis=1, keepdims=True), (TILE, HD))
-
         shift = jnp.concatenate([top[...]] * (TILE // HD), axis=1)
         mix = None
         weight_sum = None
-        for t in range(0, CHUNK, TILE):
+        for n, t in enumerate(range(0, CHUNK, TILE)):
             at = pl.ds(pl.multiple_of(i * CHUNK + t, TILE), TILE)
             p = jnp.exp2(dot_t(qrow[...], kbuf[at]) * scale - shift)
             part = dot(p.astype(bf16), vbuf[at])
             part_sum = sum(p[:, u : u + HD] for u in range(0, TILE, HD))
             mix = part if mix is None else mix + part
             weight_sum = part_sum if weight_sum is None else weight_sum + part_sum
+            if n in stages:
+                stages[n]()
         acc[...] += mix
         total[...] += weight_sum
+
+    chunk_step(0, ())
+
+    def later_step(i, unused):
+        chunk_step(i, [(i - 1) * per_step + n for n in range(per_step)])
         return 0
 
-    lax.fori_loop(0, chunks, chunk_step, 0)
+    lax.fori_loop(1, chunks, later_step, 0)
     total[...] = lane_sum(total[...])
 
     @pl.when(jnp.logical_not(jnp.max(total[...]) < SAFE_SUM))
@@ -144,57 +237,16 @@
 
         lax.fori_loop(0, rows // TILE, safe_rows, 0)
 
-    tokens = 2
-    pad = 16
-    pick_row = lax.broadcasted_iota(jnp.int32, (pad, req_rows), 0)
-    pick_col = lax.broadcasted_iota(jnp.int32, (pad, req_rows), 1)
-    put_row = lax.broadcasted_iota(jnp.int32, (req_rows, pad), 0)
-    put_col = lax.broadcasted_iota(jnp.int32, (req_rows, pad), 1)
-    pick_at = jnp.full((pad, req_rows), -1, jnp.int32)
-    put_at = jnp.full((req_rows, pad), -1, jnp.int32)
+    oslot[...] = jnp.zeros_like(oslot)
+    lslot[...] = jnp.zeros_like(lslot)
     for s in range(slot_count):
-        row = slots_ref[s] * tokens
-        pick_at = jnp.where(pick_row // tokens == s, row + pick_row % tokens, pick_at)
-        put_at = jnp.where(put_col // tokens == s, row + put_col % tokens, put_at)
-    pick = jnp.where(pick_at == pick_col, 1.0, 0.0).astype(bf16)
+        for g in range(groups):
+            put_rows = slice(s * TOKENS, (s + 1) * TOKENS)
+            lanes = slice(g * HD, (g + 1) * HD)
+            oslot[put_rows, lanes] = oraw[s, g * TOKENS : (g + 1) * TOKENS]
+            lslot[put_rows, lanes] = lraw[s, g * TOKENS : (g + 1) * TOKENS]
     put_f = jnp.where(put_at == put_row, 1.0, 0.0)
     put = put_f.astype(bf16)
-    picked = dot(pick, q_ref[...])
-    new_keys = picked[:, groups * HD : (groups + 1) * HD].astype(bf16)
-    new_values = picked[:, (groups + 1) * HD :].astype(bf16)
-    slot_rows = groups * tokens
-    for s in range(slot_count):
-        for g in range(groups):
-            qslot[s * slot_rows + g * tokens : s * slot_rows + (g + 1) * tokens] = picked[
-                s * tokens : (s + 1) * tokens, g * HD : (g + 1) * HD
-            ]
-    oslot[...] = jnp.zeros_like(oslot)
-    lslot[...] = jnp.zeros_like(lslot)
-    fresh_row = lax.broadcasted_iota(jnp.int32, (slot_rows, pad), 0)
-    fresh_col = lax.broadcasted_iota(jnp.int32, (slot_rows, pad), 1)
-    position = lax.broadcasted_iota(jnp.int32, (slot_rows, span), 1)
-    for s in range(slot_count):
-        for copy in suffix_copies(s):
-            copy.wait()
-    for s in range(slot_count):
-        q = qslot[s * slot_rows : (s + 1) * slot_rows].astype(bf16)
-        live = position < slots_ref[slot_count + s]
-        causal = (fresh_col // tokens == s) & (fresh_col % tokens <= fresh_row % tokens)
-        scores = jnp.where(live, dot_t(q, skbuf[s]) * scale, NEG_BIG)
-        fresh = jnp.where(causal, dot_t(q, new_keys) * scale, NEG_BIG)
-        high = jnp.maximum(jnp.max(scores, axis=1, keepdims=True), jnp.max(fresh, axis=1, keepdims=True))
-        p = jnp.exp2(scores - high)
-        fresh_p = jnp.exp2(fresh - high)
-        summed = jnp.sum(p, axis=1, keepdims=True) + jnp.sum(fresh_p, axis=1, keepdims=True)
-        mixed = dot(p.astype(bf16), svbuf[s]) + dot(fresh_p.astype(bf16), new_values)
-        mixed = mixed / summed
-        level = jnp.broadcast_to(high + jnp.log(summed) * LOG2E, mixed.shape)
-        for g in range(groups):
-            put_at_rows = slice(s * tokens, (s + 1) * tokens)
-            lanes = slice(g * HD, (g + 1) * HD)
-            oslot[put_at_rows, lanes] = mixed[g * tokens : (g + 1) * tokens]
-            lslot[put_at_rows, lanes] = level[g * tokens : (g + 1) * tokens]
-
     suffix_mix = sum(dot(put, piece) for piece in pieces(oslot[...]))
     suffix_level = sum(dot(put, piece) for piece in pieces(lslot[...]))
     has_suffix = jnp.sum(put_f, axis=1, keepdims=True) > 0.5
@@ -217,6 +269,45 @@
     out_ref[:, groups * HD :] = levels.astype(bf16)
 
 
+def attend(slots, gathered, prefix_k, prefix_v, suffix_k, suffix_v):
+    all_rows = gathered.shape[0]
+    width = gathered.shape[1] - 2 * HD
+    groups = width // HD
+    rows = all_rows * groups
+    slot_count = suffix_k.shape[0]
+    slot_rows = groups * TOKENS
+    chunks = prefix_k.shape[0] // CHUNK
+    vmem = pl.BlockSpec(memory_space=pltpu.VMEM)
+    smem = pl.BlockSpec(memory_space=pltpu.SMEM)
+    hbm = pl.BlockSpec(memory_space=pl.ANY)
+    return pl.pallas_call(
+        functools.partial(attend_kernel, HD**-0.5 * LOG2E),
+        in_specs=[smem, vmem, hbm, hbm, hbm, hbm],
+        out_specs=vmem,
+        out_shape=pltpu.VMEM((all_rows, width + HD), bf16),
+        scratch_shapes=[
+            pltpu.VMEM(prefix_k.shape, bf16),
+            pltpu.VMEM(prefix_v.shape, bf16),
+            pltpu.VMEM(suffix_k.shape, bf16),
+            pltpu.VMEM(suffix_v.shape, bf16),
+            pltpu.VMEM((rows, HD), bf16),
+            pltpu.VMEM((rows, HD), f32),
+            pltpu.VMEM((rows, HD), f32),
+            pltpu.VMEM((rows, HD), f32),
+            pltpu.VMEM((slot_count * slot_rows, HD), f32),
+            pltpu.VMEM((slot_count, slot_rows, HD), f32),
+            pltpu.VMEM((slot_count, slot_rows, HD), f32),
+            pltpu.VMEM((PAD, width), f32),
+            pltpu.VMEM((PAD, width), f32),
+            pltpu.SemaphoreType.DMA((chunks,)),
+            pltpu.SemaphoreType.DMA((chunks,)),
+            pltpu.SemaphoreType.DMA((2, slot_count)),
+        ],
+        compiler_params=pltpu.CompilerParams(vmem_limit_bytes=56 * 1024 * 1024),
+        name="attend",
+    )(slots, pltpu.with_memory_space_constraint(gathered, pltpu.VMEM), prefix_k, prefix_v, suffix_k, suffix_v)
+
+
 def merge_kernel(sources, copies, part_ref, out_ref):
     rows = part_ref.shape[0]
     home_rows = rows // sources
@@ -243,14 +334,12 @@
     all_rows = ctx_count * home_rows
     rows = all_rows * groups
     vmem = pl.BlockSpec(memory_space=pltpu.VMEM)
-    smem = pl.BlockSpec(memory_space=pltpu.SMEM)
-    hbm = pl.BlockSpec(memory_space=pl.ANY)
 
     sent = pl.pallas_call(
         functools.partial(spread_kernel, ctx_count),
         in_specs=[vmem] * 3,
         out_specs=vmem,
-        out_shape=jax.ShapeDtypeStruct((all_rows, width + 2 * HD), bf16),
+        out_shape=pltpu.VMEM((all_rows, width + 2 * HD), bf16),
         name="spread",
     )(queries, new_k, new_v)
     gathered = lax.all_to_all(sent, "ctx", split_axis=0, concat_axis=0, tiled=True)
@@ -262,40 +351,16 @@
     slot_length = jnp.sum(jnp.where(incoming, suffix_len[None, :], 0), axis=1)
     slots = jnp.concatenate([slot_request, slot_length])
 
-    chunks = prefix_k.shape[0] // CHUNK
-    parts = pl.pallas_call(
-        functools.partial(attend_kernel, HD**-0.5 * LOG2E),
-        in_specs=[smem, vmem, hbm, hbm, hbm, hbm],
-        out_specs=vmem,
-        out_shape=jax.ShapeDtypeStruct((all_rows, width + HD), bf16),
-        scratch_shapes=[
-            pltpu.VMEM(prefix_k.shape, bf16),
-            pltpu.VMEM(prefix_v.shape, bf16),
-            pltpu.VMEM(suffix_k.shape, bf16),
-            pltpu.VMEM(suffix_v.shape, bf16),
-            pltpu.VMEM((rows, HD), bf16),
-            pltpu.VMEM((rows, HD), f32),
-            pltpu.VMEM((rows, HD), f32),
-            pltpu.VMEM((rows, HD), f32),
-            pltpu.VMEM((slot_count * groups * tokens, HD), f32),
-            pltpu.VMEM((16, width), f32),
-            pltpu.VMEM((16, width), f32),
-            pltpu.SemaphoreType.DMA((chunks,)),
-            pltpu.SemaphoreType.DMA((chunks,)),
-            pltpu.SemaphoreType.DMA((2, slot_count)),
-        ],
-        compiler_params=pltpu.CompilerParams(vmem_limit_bytes=56 * 1024 * 1024),
-        name="attend",
-    )(slots, gathered, prefix_k, prefix_v, suffix_k, suffix_v)
+    parts = attend(slots, gathered, prefix_k, prefix_v, suffix_k, suffix_v)
     arrived = lax.all_to_all(parts, "ctx", split_axis=0, concat_axis=0, tiled=True)
 
     finished = pl.pallas_call(
         functools.partial(merge_kernel, ctx_count, head_count),
         in_specs=[vmem],
         out_specs=vmem,
-        out_shape=jax.ShapeDtypeStruct((head_count * home_rows, width), bf16),
+        out_shape=pltpu.VMEM((head_count * home_rows, width), bf16),
         name="merge",
-    )(arrived)
+    )(pltpu.with_memory_space_constraint(arrived, pltpu.VMEM))
     heads = lax.all_to_all(finished, "head", split_axis=0, concat_axis=0, tiled=True)
     heads = heads.reshape(head_count, home_rows, width).transpose(1, 0, 2)
     return heads.reshape(req_local, tokens, head_count * width)

time: 189 us -> 182 us (0.963)
  Pallas kernels: 33.9 us -> 27.4 us
    pallas_call x1, Pallas kernels: 30.5 us -> 25.7 us  [attend(): pl.pallas_call(functools.partial(attend_kernel, HD ** (-0.5) * LOG2E), in...]
where the time goes in v1:
time: 182 us
  blocking collectives  138 us (76%)
  Pallas kernels  27.4 us (15%)
  waiting for transfers between devices  7.26 us (4%)
  starting transfers between devices  6.51 us (4%)
    all_to_all x1, blocking collectives, on_device(): lax.all_to_all(parts, 'ctx', split_axis=0, concat_axis=0, tiled=True)  124 us
    pallas_call x1, Pallas kernels, attend(): pl.pallas_call(functools.partial(attend_kernel, HD ** (-0.5) * LOG2E), in...  25.7 us
    all_to_all x1, blocking collectives, on_device(): lax.all_to_all(finished, 'head', split_axis=0, concat_axis=0, tiled=True)  14.5 us
    all_to_all x1, waiting for transfers between devices, on_device(): lax.all_to_all(sent, 'ctx', split_axis=0, concat_axis=0, tiled=True)  7.26 us
    all_to_all x1, starting transfers between devices, on_device(): lax.all_to_all(sent, 'ctx', split_axis=0, concat_axis=0, tiled=True)  6.51 us
  transfers between devices with their start and end apart: 1, of which 1 were waited for; matrix products, arithmetic and copies ran while one was open for 1% of the time, Pallas kernels for 0%

profile of v1, /device:TPU:0, one launch (start us, length us, event | category | flops | bytes accessed | tf_op | source)
XLA Modules:
  0.0 181.6 jit_solution(10649920501185907882)
XLA Ops:
  0.0 1.5 spread.1
  1.5 6.5 %all-to-all-start = ((bf16[16,8,1280]{2,1,0:T(8,128)(2,1)}), bf16[16,8,1280]{2,1,0:T(8,128)(2,1)S(1)}, u32[]{:S(2)}, u32[]{:S(2)}) async-start(bf16[16,8,1280]{2,1,0:T(8,128)(2,1)} %bitcast), calls=%async_computation | async-start | bytes 655360 | tf_op jit(solution)/shard_map/all_to_all | solution.py:345
  8.0 0.9 fusion
  8.9 0.6 pad_add_fusion.slots_ref
  9.5 7.3 %all-to-all-done = bf16[16,8,1280]{2,1,0:T(8,128)(2,1)S(1)} async-done(((bf16[16,8,1280]{2,1,0:T(8,128)(2,1)}), bf16[16,8,1280]{2,1,0:T(8,128)(2,1)S(1)}, u32[]{:S(2)}, u32[]{:S(2)}) %all-to-all-start) | async-done | bytes 327712 | tf_op jit(solution)/shard_map/all_to_all | solution.py:345
  16.7 25.7 %attend.1 = bf16[128,1152]{1,0:T(8,128)(2,1)S(1)} custom-call(s32[12]{0:T(128)} %pad_add_fusion.slots_ref, bf16[128,1280]{1,0:T(8,128)(2,1)S(1)} %bitcast.6, bf16[16384,128]{1,0:T(8,128)(2,1)} %pk_ref.1, bf16[16384,128]{1,0:T(8,128)(2,1)} %pv_ref.1, bf16[6,4096,128]{2,1,0:T(8,128)(2,1)} %sk_ref.1, bf16[6,4096,128]{2,1,0:T(8,128)(2,1)} %sv_ref.1), custom_call_target="tpu_custom_call" | custom-call | tf_op jit(solution)/shard_map/attend/pallas_call | solution.py:283
  42.4 123.6 %all_to_all.31 = bf16[16,8,1152]{2,1,0:T(8,128)(2,1)S(1)} all-to-all(bf16[16,8,1152]{2,1,0:T(8,128)(2,1)S(1)} %bitcast.8), channel_id=1, replica_groups=mesh['ctx'=16,'head'=8] {'ctx'}, dimensions={0} | all-to-all | bytes 589824 | tf_op jit(solution)/shard_map/all_to_all | solution.py:355
  166.0 0.3 merge.1
  166.3 14.5 %all_to_all.32 = bf16[8,8,1024]{2,1,0:T(8,128)(2,1)S(1)} all-to-all(bf16[8,8,1024]{2,1,0:T(8,128)(2,1)S(1)} %bitcast.9), channel_id=1, replica_groups=mesh['ctx'=16,'head'=8] {'head'}, dimensions={0} | all-to-all | bytes 262144 | tf_op jit(solution)/shard_map/all_to_all | solution.py:364
  180.8 0.1 copy.11
  180.9 0.7 reshape.17
  (1 shorter events, 0.0 us)
Async XLA Ops:
  1.5 15.3 %all-to-all-start = ((bf16[16,8,1280]{2,1,0:T(8,128)(2,1)}), bf16[16,8,1280]{2,1,0:T(8,128)(2,1)S(1)}, u32[]{:S(2)}, u32[]{:S(2)}) async-start(bf16[16,8,1280]{2,1,0:T(8,128)(2,1)} %bitcast), calls=%async_computation | async-start | bytes 655360 | tf_op jit(solution)/shard_map/all_to_all | solution.py:345

commit v2 on v1

--- a/solution.py
+++ b/solution.py
@@ -18,7 +18,8 @@
 PAD = 16
 CHUNK = 4096
 TILE = 256
-SUFFIX_AT = (1, 5, 9)
+ROWBLK = 256
+KEYBLK = 1024
 
 f32 = jnp.float32
 bf16 = jnp.bfloat16
@@ -30,6 +31,10 @@
 
 def dot_t(a, b):
     return lax.dot_general(a, b, (((1,), (1,)), ((), ())), preferred_element_type=f32)
+
+
+def near(x):
+    return pltpu.with_memory_space_constraint(x, pltpu.VMEM)
 
 
 def lane_sum(x):
@@ -44,7 +49,7 @@
     return first, second, third
 
 
-def spread_kernel(copies, q_ref, k_ref, v_ref, out_ref):
+def spread_kernel(copies, q_ref, k_ref, v_ref, owner_ref, length_ref, out_ref, table_ref):
     rows = q_ref.shape[0] * q_ref.shape[1]
     width = q_ref.shape[2]
     block = jnp.concatenate(
@@ -56,11 +61,13 @@
         axis=1,
     )
     out_ref[...] = jnp.concatenate([block] * copies, axis=0).astype(bf16)
+    table_ref[0:1] = owner_ref[...]
+    table_ref[1:2] = length_ref[...]
 
 
 def attend_kernel(
-    scale, slots_ref, q_ref, pk_ref, pv_ref, sk_ref, sv_ref, out_ref,
-    kbuf, vbuf, skbuf, svbuf, qrow, top, acc, total, qslot, oraw, lraw, oslot, lslot, ksem, vsem, ssem,
+    scale, table_ref, q_ref, pk_ref, pv_ref, sk_ref, sv_ref, out_ref,
+    kbuf, vbuf, vturn, skbuf, svbuf, qrow, top, acc, total, qslot, oraw, lraw, oslot, lslot, ksem, vsem, ssem,
 ):
     req_rows = q_ref.shape[0]
     groups = (q_ref.shape[1] - 2 * HD) // HD
@@ -91,17 +98,18 @@
     acc[...] = jnp.zeros_like(acc)
     total[...] = jnp.zeros_like(total)
 
+    requests = table_ref.shape[1]
+    base = lax.axis_index("ctx") * slot_count
+    slot_of = lax.broadcasted_iota(jnp.int32, (PAD, requests), 0) // TOKENS
+    owned = (table_ref[0:1] == base + slot_of) & (slot_of < slot_count)
+    lengths = jnp.sum(jnp.where(owned, table_ref[1:2], 0), axis=1, keepdims=True)
+    spread_row = lax.broadcasted_iota(jnp.int32, (requests, req_rows), 0)
+    spread_col = lax.broadcasted_iota(jnp.int32, (requests, req_rows), 1)
+    spread = jnp.where(spread_col // TOKENS == spread_row, 1.0, 0.0).astype(bf16)
     pick_row = lax.broadcasted_iota(jnp.int32, (PAD, req_rows), 0)
     pick_col = lax.broadcasted_iota(jnp.int32, (PAD, req_rows), 1)
-    put_row = lax.broadcasted_iota(jnp.int32, (req_rows, PAD), 0)
-    put_col = lax.broadcasted_iota(jnp.int32, (req_rows, PAD), 1)
-    pick_at = jnp.full((PAD, req_rows), -1, jnp.int32)
-    put_at = jnp.full((req_rows, PAD), -1, jnp.int32)
-    for s in range(slot_count):
-        row = slots_ref[s] * TOKENS
-        pick_at = jnp.where(pick_row // TOKENS == s, row + pick_row % TOKENS, pick_at)
-        put_at = jnp.where(put_col // TOKENS == s, row + put_col % TOKENS, put_at)
-    pick = jnp.where(pick_at == pick_col, 1.0, 0.0).astype(bf16)
+    pick = dot(jnp.where(owned, 1.0, 0.0).astype(bf16), spread)
+    pick = jnp.where(pick_row % TOKENS == pick_col % TOKENS, pick, 0.0).astype(bf16)
     picked = dot(pick, q_ref[...])
     new_keys = picked[:, groups * HD : (groups + 1) * HD].astype(bf16)
     new_values = picked[:, (groups + 1) * HD :].astype(bf16)
@@ -134,7 +142,7 @@
             causal = blocks(
                 lambda s: (fresh_col // TOKENS == s) & (fresh_col % TOKENS <= fresh_row % TOKENS)
             )
-            live = blocks(lambda s: position < slots_ref[slot_count + s])
+            live = blocks(lambda s: position < lengths[s * TOKENS : s * TOKENS + 1])
             keys = jnp.concatenate([skbuf[s] for s in slots], axis=1)
             held["scores"] = jnp.where(live, dot_t(apart(q).astype(bf16), keys) * scale, NEG_BIG)
             held["fresh"] = jnp.where(causal, dot_t(q.astype(bf16), new_keys) * scale, NEG_BIG)
@@ -162,81 +170,93 @@
 
         return [score, weigh, mix]
 
-    def chunk_step(i, slots):
-        stages = {}
-        for copy in prefix_copies(i):
-            copy.wait()
-        if slots:
-            for s in slots:
-                for copy in suffix_copies(s):
-                    copy.wait()
-            stages = dict(zip(SUFFIX_AT, suffix_stages(slots)))
-
-        def start_next():
-            for copy in prefix_copies(i + 1):
+    def first_top():
+        for r in range(0, rows, ROWBLK):
+            high = jnp.max(dot_t(kbuf[0:TILE], qrow[r : r + ROWBLK]), axis=0, keepdims=True) * scale
+            top[:, r : r + ROWBLK] = jnp.broadcast_to(high, (8, ROWBLK))
+
+    def start_next(i):
+        for copy in prefix_copies(i + 1):
+            copy.start()
+        for n in range(per_step):
+            for copy in suffix_copies(i * per_step + n):
                 copy.start()
-            for n in range(per_step):
-                for copy in suffix_copies(i * per_step + n):
-                    copy.start()
-
-        if slots:
-            pl.when(i + 1 < chunks)(start_next)
-        else:
-            start_next()
-            for r in range(0, rows, TILE):
-                s = dot_t(qrow[r : r + TILE], kbuf[0:TILE]) * scale
-                top[r : r + TILE] = jnp.broadcast_to(jnp.max(s, axis=1, keepdims=True), (TILE, HD))
-        shift = jnp.concatenate([top[...]] * (TILE // HD), axis=1)
-        mix = None
-        weight_sum = None
-        for n, t in enumerate(range(0, CHUNK, TILE)):
-            at = pl.ds(pl.multiple_of(i * CHUNK + t, TILE), TILE)
-            p = jnp.exp2(dot_t(qrow[...], kbuf[at]) * scale - shift)
-            part = dot(p.astype(bf16), vbuf[at])
-            part_sum = sum(p[:, u : u + HD] for u in range(0, TILE, HD))
-            mix = part if mix is None else mix + part
-            weight_sum = part_sum if weight_sum is None else weight_sum + part_sum
-            if n in stages:
-                stages[n]()
-        acc[...] += mix
-        total[...] += weight_sum
-
-    chunk_step(0, ())
-
-    def later_step(i, unused):
-        chunk_step(i, [(i - 1) * per_step + n for n in range(per_step)])
+
+    def wait_suffix(i):
+        for n in range(per_step):
+            for copy in suffix_copies(i * per_step + n):
+                copy.wait()
+
+    def prefix_chunk(i):
+        vturn[...] = jnp.transpose(vbuf[pl.ds(pl.multiple_of(i * CHUNK, CHUNK), CHUNK)])
+        blocks = [(r, t) for r in range(0, rows, ROWBLK) for t in range(0, CHUNK, KEYBLK)]
+
+        def score(block):
+            r, t = block
+            keys = pl.ds(pl.multiple_of(i * CHUNK + t, KEYBLK), KEYBLK)
+            return dot_t(kbuf[keys], qrow[r : r + ROWBLK])
+
+        ready = score(blocks[0])
+        mix = weight_sum = None
+        for n, (r, t) in enumerate(blocks):
+            scores = ready
+            if n + 1 < len(blocks):
+                ready = score(blocks[n + 1])
+            p = jnp.exp2(scores * scale - top[0:1, r : r + ROWBLK])
+            part = dot(vturn[:, t : t + KEYBLK], p.astype(bf16))
+            part_sum = jnp.sum(p.reshape(KEYBLK // 8, 8, ROWBLK), axis=0)
+            mix = part if t == 0 else mix + part
+            weight_sum = part_sum if t == 0 else weight_sum + part_sum
+            if t + KEYBLK == CHUNK:
+                acc[:, r : r + ROWBLK] += mix
+                total[:, r : r + ROWBLK] += weight_sum
+
+    def step(i, unused):
+        keys_copy, values_copy = prefix_copies(i)
+        keys_copy.wait()
+        pl.when(i + 1 < chunks)(lambda: start_next(i))
+        pl.when(i == 0)(first_top)
+        values_copy.wait()
+        prefix_chunk(i)
         return 0
 
-    lax.fori_loop(1, chunks, later_step, 0)
-    total[...] = lane_sum(total[...])
-
-    @pl.when(jnp.logical_not(jnp.max(total[...]) < SAFE_SUM))
+    lax.fori_loop(0, chunks, step, 0)
+    summed = jnp.sum(total[...], axis=0, keepdims=True)
+    total[...] = jnp.broadcast_to(summed, total.shape)
+
+    @pl.when(jnp.logical_not(jnp.max(summed) < SAFE_SUM))
     def _():
         def safe_rows(j, unused):
-            at = pl.ds(pl.multiple_of(j * TILE, TILE), TILE)
+            at = pl.ds(pl.multiple_of(j * ROWBLK, ROWBLK), ROWBLK)
             q = qrow[at]
 
             def safe_keys(i, carried):
                 high, summed, mixed = carried
                 keys = pl.ds(pl.multiple_of(i * TILE, TILE), TILE)
-                s = dot_t(q, kbuf[keys]) * scale
-                new = jnp.maximum(high, jnp.broadcast_to(jnp.max(s, axis=1, keepdims=True), high.shape))
-                p = jnp.exp2(s - jnp.concatenate([new] * (TILE // HD), axis=1))
+                s = dot_t(kbuf[keys], q) * scale
+                new = jnp.maximum(high, jnp.max(s, axis=0, keepdims=True))
+                p = jnp.exp2(s - new)
                 decay = jnp.exp2(high - new)
-                part = jnp.broadcast_to(jnp.sum(p, axis=1, keepdims=True), high.shape)
-                return new, summed * decay + part, mixed * decay + dot(p.astype(bf16), vbuf[keys])
-
-            zero = jnp.zeros((TILE, HD), f32)
+                summed = summed * decay + jnp.sum(p, axis=0, keepdims=True)
+                return new, summed, mixed * decay + dot(jnp.transpose(vbuf[keys]), p.astype(bf16))
+
+            zero = jnp.zeros((1, ROWBLK), f32)
             high, summed, mixed = lax.fori_loop(
-                0, chunks * CHUNK // TILE, safe_keys, (zero + NEG_BIG, zero, zero)
+                0, chunks * CHUNK // TILE, safe_keys, (zero + NEG_BIG, zero, jnp.zeros((HD, ROWBLK), f32))
             )
-            top[at] = high
-            total[at] = summed
-            acc[at] = mixed
+            top[:, at] = jnp.broadcast_to(high, (8, ROWBLK))
+            total[:, at] = jnp.broadcast_to(summed, (8, ROWBLK))
+            acc[:, at] = mixed
             return 0
 
-        lax.fori_loop(0, rows // TILE, safe_rows, 0)
-
+        lax.fori_loop(0, rows // ROWBLK, safe_rows, 0)
+
+    for i in range(chunks - 1):
+        wait_suffix(i)
+    staged = [suffix_stages([i * per_step + n for n in range(per_step)]) for i in range(chunks - 1)]
+    for m in range(3):
+        for stages in staged:
+            stages[m]()
     oslot[...] = jnp.zeros_like(oslot)
     lslot[...] = jnp.zeros_like(lslot)
     for s in range(slot_count):
@@ -245,7 +265,9 @@
             lanes = slice(g * HD, (g + 1) * HD)
             oslot[put_rows, lanes] = oraw[s, g * TOKENS : (g + 1) * TOKENS]
             lslot[put_rows, lanes] = lraw[s, g * TOKENS : (g + 1) * TOKENS]
-    put_f = jnp.where(put_at == put_row, 1.0, 0.0)
+    same_row = lax.broadcasted_iota(jnp.int32, (req_rows, req_rows), 0)
+    same_col = lax.broadcasted_iota(jnp.int32, (req_rows, req_rows), 1)
+    put_f = dot_t(jnp.where(same_row == same_col, 1.0, 0.0).astype(bf16), pick)
     put = put_f.astype(bf16)
     suffix_mix = sum(dot(put, piece) for piece in pieces(oslot[...]))
     suffix_level = sum(dot(put, piece) for piece in pieces(lslot[...]))
@@ -255,13 +277,15 @@
     for g in range(groups):
         at = slice(g * req_rows, (g + 1) * req_rows)
         lanes = slice(g * HD, (g + 1) * HD)
-        level = top[at] + jnp.log(total[at]) * LOG2E
+        level = top[0:1, at] + jnp.log(total[0:1, at]) * LOG2E
+        level = jnp.transpose(jnp.broadcast_to(level, (HD, req_rows)))
+        prefix_mix = jnp.transpose(acc[:, at] / total[0:1, at])
         other = jnp.where(has_suffix, suffix_level[:, lanes], NEG_BIG)
         high = jnp.maximum(level, other)
         mine = jnp.exp2(level - high)
         theirs = jnp.exp2(other - high)
         summed = mine + theirs
-        mixed = (acc[at] / total[at] * mine + suffix_mix[:, lanes] * theirs) / summed
+        mixed = (prefix_mix * mine + suffix_mix[:, lanes] * theirs) / summed
         out_ref[:, lanes] = mixed.astype(bf16)
         level = high + jnp.log(summed) * LOG2E
         for j, piece in enumerate(pieces(level)):
@@ -269,7 +293,7 @@
     out_ref[:, groups * HD :] = levels.astype(bf16)
 
 
-def attend(slots, gathered, prefix_k, prefix_v, suffix_k, suffix_v):
+def attend(table, gathered, prefix_k, prefix_v, suffix_k, suffix_v):
     all_rows = gathered.shape[0]
     width = gathered.shape[1] - 2 * HD
     groups = width // HD
@@ -278,22 +302,22 @@
     slot_rows = groups * TOKENS
     chunks = prefix_k.shape[0] // CHUNK
     vmem = pl.BlockSpec(memory_space=pltpu.VMEM)
-    smem = pl.BlockSpec(memory_space=pltpu.SMEM)
     hbm = pl.BlockSpec(memory_space=pl.ANY)
     return pl.pallas_call(
         functools.partial(attend_kernel, HD**-0.5 * LOG2E),
-        in_specs=[smem, vmem, hbm, hbm, hbm, hbm],
+        in_specs=[vmem, vmem, hbm, hbm, hbm, hbm],
         out_specs=vmem,
         out_shape=pltpu.VMEM((all_rows, width + HD), bf16),
         scratch_shapes=[
             pltpu.VMEM(prefix_k.shape, bf16),
             pltpu.VMEM(prefix_v.shape, bf16),
+            pltpu.VMEM((HD, CHUNK), bf16),
             pltpu.VMEM(suffix_k.shape, bf16),
             pltpu.VMEM(suffix_v.shape, bf16),
             pltpu.VMEM((rows, HD), bf16),
-            pltpu.VMEM((rows, HD), f32),
-            pltpu.VMEM((rows, HD), f32),
-            pltpu.VMEM((rows, HD), f32),
+            pltpu.VMEM((8, rows), f32),
+            pltpu.VMEM((HD, rows), f32),
+            pltpu.VMEM((8, rows), f32),
             pltpu.VMEM((slot_count * slot_rows, HD), f32),
             pltpu.VMEM((slot_count, slot_rows, HD), f32),
             pltpu.VMEM((slot_count, slot_rows, HD), f32),
@@ -305,7 +329,14 @@
         ],
         compiler_params=pltpu.CompilerParams(vmem_limit_bytes=56 * 1024 * 1024),
         name="attend",
-    )(slots, pltpu.with_memory_space_constraint(gathered, pltpu.VMEM), prefix_k, prefix_v, suffix_k, suffix_v)
+    )(
+        near(table),
+        near(gathered),
+        prefix_k,
+        prefix_v,
+        suffix_k,
+        suffix_v,
+    )
 
 
 def merge_kernel(sources, copies, part_ref, out_ref):
@@ -326,32 +357,26 @@
 def on_device(queries, prefix_k, prefix_v, suffix_k, suffix_v, new_k, new_v, suffix_len, owner_of):
     req_local, tokens, width = queries.shape
     groups = width // HD
-    slot_count, span = suffix_k.shape[0], suffix_k.shape[1]
     ctx_count = lax.axis_size("ctx")
     head_count = lax.axis_size("head")
-    ctx_index = lax.axis_index("ctx")
     home_rows = req_local * tokens
     all_rows = ctx_count * home_rows
     rows = all_rows * groups
     vmem = pl.BlockSpec(memory_space=pltpu.VMEM)
 
-    sent = pl.pallas_call(
+    sent, table = pl.pallas_call(
         functools.partial(spread_kernel, ctx_count),
-        in_specs=[vmem] * 3,
-        out_specs=vmem,
-        out_shape=pltpu.VMEM((all_rows, width + 2 * HD), bf16),
+        in_specs=[vmem] * 5,
+        out_specs=[vmem] * 2,
+        out_shape=[
+            pltpu.VMEM((all_rows, width + 2 * HD), bf16),
+            pltpu.VMEM((2, owner_of.shape[0]), jnp.int32),
+        ],
         name="spread",
-    )(queries, new_k, new_v)
+    )(queries, new_k, new_v, owner_of.reshape(1, -1), suffix_len.reshape(1, -1))
     gathered = lax.all_to_all(sent, "ctx", split_axis=0, concat_axis=0, tiled=True)
 
-    my_slots = ctx_index * slot_count + jnp.arange(slot_count, dtype=jnp.int32)
-    incoming = owner_of[None, :] == my_slots[:, None]
-    request = jnp.arange(owner_of.shape[0], dtype=jnp.int32)
-    slot_request = jnp.max(jnp.where(incoming, request[None, :], -4), axis=1)
-    slot_length = jnp.sum(jnp.where(incoming, suffix_len[None, :], 0), axis=1)
-    slots = jnp.concatenate([slot_request, slot_length])
-
-    parts = attend(slots, gathered, prefix_k, prefix_v, suffix_k, suffix_v)
+    parts = attend(table, gathered, prefix_k, prefix_v, suffix_k, suffix_v)
     arrived = lax.all_to_all(parts, "ctx", split_axis=0, concat_axis=0, tiled=True)
 
     finished = pl.pallas_call(
@@ -360,7 +385,7 @@
         out_specs=vmem,
         out_shape=pltpu.VMEM((head_count * home_rows, width), bf16),
         name="merge",
-    )(pltpu.with_memory_space_constraint(arrived, pltpu.VMEM))
+    )(near(arrived))
     heads = lax.all_to_all(finished, "head", split_axis=0, concat_axis=0, tiled=True)
     heads = heads.reshape(head_count, home_rows, width).transpose(1, 0, 2)
     return heads.reshape(req_local, tokens, head_count * width)

time: 182 us -> 177 us (0.973)
  blocking collectives: 138 us -> 153 us
  waiting for transfers between devices: 7.26 us -> 0 us
  starting transfers between devices: 6.51 us -> 0 us
  Pallas kernels: 27.4 us -> 23.1 us
    all_to_all x0 -> x1, blocking collectives: none -> 15.1 us  [on_device(): lax.all_to_all(sent, 'ctx', split_axis=0, concat_axis=0, tiled=True)]
    all_to_all x1 -> x0, waiting for transfers between devices: 7.26 us -> none  [on_device(): lax.all_to_all(sent, 'ctx', split_axis=0, concat_axis=0, tiled=True)]
    all_to_all x1 -> x0, starting transfers between devices: 6.51 us -> none  [on_device(): lax.all_to_all(sent, 'ctx', split_axis=0, concat_axis=0, tiled=True)]
    pallas_call x1, Pallas kernels: 25.7 us -> 22.1 us  [attend(): pl.pallas_call(functools.partial(attend_kernel, HD ** (-0.5) * LOG2E), in...]
  transfers between devices with their start and end apart: 1 -> 0, of which waited for: 1 -> 0; matrix products, arithmetic and copies ran while one was open for 1% -> 0% of each run, Pallas kernels for 0% -> 0%
where the time goes in v2:
time: 177 us
  blocking collectives  153 us (86%)
  Pallas kernels  23.1 us (13%)
    all_to_all x1, blocking collectives, on_device(): lax.all_to_all(parts, 'ctx', split_axis=0, concat_axis=0, tiled=True)  123 us
    pallas_call x1, Pallas kernels, attend(): pl.pallas_call(functools.partial(attend_kernel, HD ** (-0.5) * LOG2E), in...  22.1 us
    all_to_all x1, blocking collectives, on_device(): lax.all_to_all(sent, 'ctx', split_axis=0, concat_axis=0, tiled=True)  15.1 us
    all_to_all x1, blocking collectives, on_device(): lax.all_to_all(finished, 'head', split_axis=0, concat_axis=0, tiled=True)  14.5 us

profile of v2, /device:TPU:0, one launch (start us, length us, event | category | flops | bytes accessed | tf_op | source)
XLA Modules:
  0.0 176.6 jit_solution(3445022067397996314)
XLA Ops:
  0.0 0.8 spread.1
  0.8 15.1 %all_to_all.31 = bf16[16,8,1280]{2,1,0:T(8,128)(2,1)S(1)} all-to-all(bf16[16,8,1280]{2,1,0:T(8,128)(2,1)S(1)} %bitcast.12), channel_id=1, replica_groups=mesh['ctx'=16,'head'=8] {'ctx'}, dimensions={0} | all-to-all | bytes 655360 | tf_op jit(solution)/shard_map/all_to_all | solution.py:377
  15.9 22.1 %attend.1 = bf16[128,1152]{1,0:T(8,128)(2,1)S(1)} custom-call(s32[2,64]{1,0:T(2,128)S(1)} %get-tuple-element.7.table_ref, bf16[128,1280]{1,0:T(8,128)(2,1)S(1)} %bitcast.8, bf16[16384,128]{1,0:T(8,128)(2,1)} %pk_ref.1, bf16[16384,128]{1,0:T(8,128)(2,1)} %pv_ref.1, bf16[6,4096,128]{2,1,0:T(8,128)(2,1)} %sk_ref.1, bf16[6,4096,128]{2,1,0:T(8,128)(2,1)} %sv_ref.1), custom_call_target="tpu_custom_call" | custom-call | tf_op jit(solution)/shard_map/attend/pallas_call | solution.py:306
  38.0 123.0 %all_to_all.32 = bf16[16,8,1152]{2,1,0:T(8,128)(2,1)S(1)} all-to-all(bf16[16,8,1152]{2,1,0:T(8,128)(2,1)S(1)} %bitcast.10), channel_id=1, replica_groups=mesh['ctx'=16,'head'=8] {'ctx'}, dimensions={0} | all-to-all | bytes 589824 | tf_op jit(solution)/shard_map/all_to_all | solution.py:380
  161.0 0.3 merge.1
  161.3 14.5 %all_to_all.33 = bf16[8,8,1024]{2,1,0:T(8,128)(2,1)S(1)} all-to-all(bf16[8,8,1024]{2,1,0:T(8,128)(2,1)S(1)} %bitcast.11), channel_id=1, replica_groups=mesh['ctx'=16,'head'=8] {'head'}, dimensions={0} | all-to-all | bytes 262144 | tf_op jit(solution)/shard_map/all_to_all | solution.py:389
  175.8 0.1 copy.10
  175.9 0.7 reshape.19

commit v3 on v2

--- a/solution.py
+++ b/solution.py
@@ -49,28 +49,28 @@
     return first, second, third
 
 
-def spread_kernel(copies, q_ref, k_ref, v_ref, owner_ref, length_ref, out_ref, table_ref):
+def previous_row(x):
+    return jnp.concatenate([x[-1:], x[:-1]], axis=0)
+
+
+def spread_kernel(copies, q_ref, k_ref, v_ref, owner_ref, length_ref, out_ref, home_ref, table_ref):
     rows = q_ref.shape[0] * q_ref.shape[1]
     width = q_ref.shape[2]
-    block = jnp.concatenate(
-        [
-            q_ref[...].astype(f32).reshape(rows, width),
-            k_ref[...].astype(f32).reshape(rows, HD),
-            v_ref[...].astype(f32).reshape(rows, HD),
-        ],
-        axis=1,
-    )
+    block = q_ref[...].astype(f32).reshape(rows, width)
     out_ref[...] = jnp.concatenate([block] * copies, axis=0).astype(bf16)
+    home_ref[:, :width] = block
+    home_ref[:, width : width + HD] = k_ref[...].astype(f32).reshape(rows, HD)
+    home_ref[:, width + HD :] = v_ref[...].astype(f32).reshape(rows, HD)
     table_ref[0:1] = owner_ref[...]
     table_ref[1:2] = length_ref[...]
 
 
 def attend_kernel(
-    scale, table_ref, q_ref, pk_ref, pv_ref, sk_ref, sv_ref, out_ref,
+    scale, table_ref, home_ref, q_ref, pk_ref, pv_ref, sk_ref, sv_ref, out_ref, fresh_ref,
     kbuf, vbuf, vturn, skbuf, svbuf, qrow, top, acc, total, qslot, oraw, lraw, oslot, lslot, ksem, vsem, ssem,
 ):
     req_rows = q_ref.shape[0]
-    groups = (q_ref.shape[1] - 2 * HD) // HD
+    groups = q_ref.shape[1] // HD
     rows = req_rows * groups
     slot_count, span = sk_ref.shape[0], sk_ref.shape[1]
     slot_rows = groups * TOKENS
@@ -97,6 +97,14 @@
         qrow[g * req_rows : (g + 1) * req_rows] = q_ref[:, g * HD : (g + 1) * HD]
     acc[...] = jnp.zeros_like(acc)
     total[...] = jnp.zeros_like(total)
+
+    key = home_ref[:, groups * HD : (groups + 1) * HD]
+    second = lax.broadcasted_iota(jnp.int32, key.shape, 0) % TOKENS == 1
+    for g in range(groups):
+        q = home_ref[:, g * HD : (g + 1) * HD]
+        fresh_ref[:, g * HD : (g + 1) * HD] = lane_sum(q * key) * scale
+        first = lane_sum(q * previous_row(key)) * scale
+        fresh_ref[:, (groups + g) * HD : (groups + g + 1) * HD] = jnp.where(second, first, NEG_BIG)
 
     requests = table_ref.shape[1]
     base = lax.axis_index("ctx") * slot_count
@@ -111,15 +119,11 @@
     pick = dot(jnp.where(owned, 1.0, 0.0).astype(bf16), spread)
     pick = jnp.where(pick_row % TOKENS == pick_col % TOKENS, pick, 0.0).astype(bf16)
     picked = dot(pick, q_ref[...])
-    new_keys = picked[:, groups * HD : (groups + 1) * HD].astype(bf16)
-    new_values = picked[:, (groups + 1) * HD :].astype(bf16)
     for s in range(slot_count):
         for g in range(groups):
             qslot[s * slot_rows + g * TOKENS : s * slot_rows + (g + 1) * TOKENS] = picked[
                 s * TOKENS : (s + 1) * TOKENS, g * HD : (g + 1) * HD
             ]
-    fresh_row = lax.broadcasted_iota(jnp.int32, (slot_rows, PAD), 0)
-    fresh_col = lax.broadcasted_iota(jnp.int32, (slot_rows, PAD), 1)
     position = lax.broadcasted_iota(jnp.int32, (slot_rows, span), 1)
 
     def suffix_stages(slots):
@@ -139,32 +143,24 @@
 
         def score():
             q = blocks(lambda s: qslot[pl.ds(pl.multiple_of(s * slot_rows, slot_rows), slot_rows)])
-            causal = blocks(
-                lambda s: (fresh_col // TOKENS == s) & (fresh_col % TOKENS <= fresh_row % TOKENS)
-            )
             live = blocks(lambda s: position < lengths[s * TOKENS : s * TOKENS + 1])
             keys = jnp.concatenate([skbuf[s] for s in slots], axis=1)
             held["scores"] = jnp.where(live, dot_t(apart(q).astype(bf16), keys) * scale, NEG_BIG)
-            held["fresh"] = jnp.where(causal, dot_t(q.astype(bf16), new_keys) * scale, NEG_BIG)
 
         def weigh():
-            scores, fresh = held["scores"], held["fresh"]
-            high = jnp.maximum(
-                jnp.max(scores, axis=1, keepdims=True), jnp.max(fresh, axis=1, keepdims=True)
-            )
+            scores = held["scores"]
+            high = jnp.max(scores, axis=1, keepdims=True)
             p = jnp.exp2(scores - high)
-            fresh_p = jnp.exp2(fresh - high)
-            held["sum"] = jnp.sum(p, axis=1, keepdims=True) + jnp.sum(fresh_p, axis=1, keepdims=True)
-            held["high"], held["p"], held["fresh_p"] = high, p.astype(bf16), fresh_p.astype(bf16)
+            held["sum"] = jnp.sum(p, axis=1, keepdims=True)
+            held["high"], held["p"] = high, p.astype(bf16)
 
         def mix():
             values = jnp.concatenate([svbuf[s] for s in slots], axis=1)
             wide = dot(held["p"], values)
-            fresh_mix = dot(held["fresh_p"], new_values)
             level = held["high"] + jnp.log(held["sum"]) * LOG2E
             for n, s in enumerate(slots):
                 at = slice(n * slot_rows, (n + 1) * slot_rows)
-                mixed = wide[at, n * HD : (n + 1) * HD] + fresh_mix[at]
+                mixed = wide[at, n * HD : (n + 1) * HD]
                 oraw[s] = mixed / held["sum"][at]
                 lraw[s] = jnp.broadcast_to(level[at], mixed.shape)
 
@@ -293,9 +289,9 @@
     out_ref[:, groups * HD :] = levels.astype(bf16)
 
 
-def attend(table, gathered, prefix_k, prefix_v, suffix_k, suffix_v):
+def attend(table, home, gathered, prefix_k, prefix_v, suffix_k, suffix_v):
     all_rows = gathered.shape[0]
-    width = gathered.shape[1] - 2 * HD
+    width = gathered.shape[1]
     groups = width // HD
     rows = all_rows * groups
     slot_count = suffix_k.shape[0]
@@ -305,9 +301,12 @@
     hbm = pl.BlockSpec(memory_space=pl.ANY)
     return pl.pallas_call(
         functools.partial(attend_kernel, HD**-0.5 * LOG2E),
-        in_specs=[vmem, vmem, hbm, hbm, hbm, hbm],
-        out_specs=vmem,
-        out_shape=pltpu.VMEM((all_rows, width + HD), bf16),
+        in_specs=[vmem, vmem, vmem, hbm, hbm, hbm, hbm],
+        out_specs=[vmem] * 2,
+        out_shape=[
+            pltpu.VMEM((all_rows, width + HD), bf16),
+            pltpu.VMEM((home.shape[0], 2 * width), f32),
+        ],
         scratch_shapes=[
             pltpu.VMEM(prefix_k.shape, bf16),
             pltpu.VMEM(prefix_v.shape, bf16),
@@ -331,6 +330,7 @@
         name="attend",
     )(
         near(table),
+        near(home),
         near(gathered),
         prefix_k,
         prefix_v,
@@ -339,18 +339,26 @@
     )
 
 
-def merge_kernel(sources, copies, part_ref, out_ref):
+def merge_kernel(sources, copies, part_ref, fresh_ref, home_ref, out_ref):
     rows = part_ref.shape[0]
     home_rows = rows // sources
     groups = (part_ref.shape[1] - HD) // HD
     levels = part_ref[:, groups * HD :].astype(f32)
     lane = lax.broadcasted_iota(jnp.int32, (rows, HD), 1)
+    value = home_ref[:, (groups + 1) * HD :]
+    first_value = previous_row(value)
     for g in range(groups):
         mine = (lane % groups == g) & (lane < 3 * groups)
         level = lane_sum(jnp.where(mine, levels, 0.0)).reshape(sources, home_rows, HD)
-        weight = jnp.exp2(level - jnp.max(level, axis=0, keepdims=True))
+        own = fresh_ref[:, g * HD : (g + 1) * HD]
+        first = fresh_ref[:, (groups + g) * HD : (groups + g + 1) * HD]
+        high = jnp.maximum(jnp.max(level, axis=0), jnp.maximum(own, first))
+        weight = jnp.exp2(level - high[None])
+        own = jnp.exp2(own - high)
+        first = jnp.exp2(first - high)
         part = part_ref[:, g * HD : (g + 1) * HD].astype(f32).reshape(sources, home_rows, HD)
-        mixed = jnp.sum(part * weight, axis=0) / jnp.sum(weight, axis=0)
+        mixed = jnp.sum(part * weight, axis=0) + own * value + first * first_value
+        mixed = mixed / (jnp.sum(weight, axis=0) + own + first)
         out_ref[:, g * HD : (g + 1) * HD] = jnp.concatenate([mixed] * copies, axis=0).astype(bf16)
 
 
@@ -364,28 +372,29 @@
     rows = all_rows * groups
     vmem = pl.BlockSpec(memory_space=pltpu.VMEM)
 
-    sent, table = pl.pallas_call(
+    sent, home, table = pl.pallas_call(
         functools.partial(spread_kernel, ctx_count),
         in_specs=[vmem] * 5,
-        out_specs=[vmem] * 2,
+        out_specs=[vmem] * 3,
         out_shape=[
-            pltpu.VMEM((all_rows, width + 2 * HD), bf16),
+            pltpu.VMEM((all_rows, width), bf16),
+            pltpu.VMEM((home_rows, width + 2 * HD), f32),
             pltpu.VMEM((2, owner_of.shape[0]), jnp.int32),
         ],
         name="spread",
     )(queries, new_k, new_v, owner_of.reshape(1, -1), suffix_len.reshape(1, -1))
     gathered = lax.all_to_all(sent, "ctx", split_axis=0, concat_axis=0, tiled=True)
 
-    parts = attend(table, gathered, prefix_k, prefix_v, suffix_k, suffix_v)
+    parts, fresh = attend(table, home, gathered, prefix_k, prefix_v, suffix_k, suffix_v)
     arrived = lax.all_to_all(parts, "ctx", split_axis=0, concat_axis=0, tiled=True)
 
     finished = pl.pallas_call(
         functools.partial(merge_kernel, ctx_count, head_count),
-        in_specs=[vmem],
+        in_specs=[vmem] * 3,
         out_specs=vmem,
         out_shape=pltpu.VMEM((head_count * home_rows, width), bf16),
         name="merge",
-    )(near(arrived))
+    )(near(arrived), near(fresh), near(home))
     heads = lax.all_to_all(finished, "head", split_axis=0, concat_axis=0, tiled=True)
     heads = heads.reshape(head_count, home_rows, width).transpose(1, 0, 2)
     return heads.reshape(req_local, tokens, head_count * width)

time: 177 us -> 176 us (level)
  blocking collectives: 153 us -> 151 us
where the time goes in v3:
time: 176 us; the launch traced here: 175 us
  blocking collectives  151 us (86%)
  Pallas kernels  23.3 us (13%)
    all_to_all x1, blocking collectives, on_device(): lax.all_to_all(parts, 'ctx', split_axis=0, concat_axis=0, tiled=True)  122 us
    pallas_call x1, Pallas kernels, attend(): pl.pallas_call(functools.partial(attend_kernel, HD ** (-0.5) * LOG2E), in...  22.2 us
    all_to_all x1, blocking collectives, on_device(): lax.all_to_all(finished, 'head', split_axis=0, concat_axis=0, tiled=True)  14.5 us
    all_to_all x1, blocking collectives, on_device(): lax.all_to_all(sent, 'ctx', split_axis=0, concat_axis=0, tiled=True)  14.4 us

profile of v3, /device:TPU:0, one launch (start us, length us, event | category | flops | bytes accessed | tf_op | source)
XLA Modules:
  0.0 175.5 jit_solution(8189576781991244548)
XLA Ops:
  0.0 0.8 spread.1
  0.8 14.4 %all_to_all.31 = bf16[16,8,1024]{2,1,0:T(8,128)(2,1)S(1)} all-to-all(bf16[16,8,1024]{2,1,0:T(8,128)(2,1)S(1)} %bitcast.12), channel_id=1, replica_groups=mesh['ctx'=16,'head'=8] {'ctx'}, dimensions={0} | all-to-all | bytes 524288 | tf_op jit(solution)/shard_map/all_to_all | solution.py:386
  15.2 22.2 %attend.1 = (bf16[128,1152]{1,0:T(8,128)(2,1)S(1)}, f32[8,2048]{1,0:T(8,128)S(1)}) custom-call(s32[2,64]{1,0:T(2,128)S(1)} %get-tuple-element.10.table_ref, f32[8,1280]{1,0:T(8,128)S(1)} %get-tuple-element.11.home_ref, bf16[128,1024]{1,0:T(8,128)(2,1)S(1)} %bitcast.9, bf16[16384,128]{1,0:T(8,128)(2,1)} %pk_ref.1, bf16[16384,128]{1,0:T(8,128)(2,1)} %pv_ref.1, ...), custom_call_target="tpu_custom_call" | custom-call | tf_op jit(solution)/shard_map/attend/pallas_call | solution.py:302
  37.4 122.5 %all_to_all.32 = bf16[16,8,1152]{2,1,0:T(8,128)(2,1)S(1)} all-to-all(bf16[16,8,1152]{2,1,0:T(8,128)(2,1)S(1)} %bitcast.11), channel_id=1, replica_groups=mesh['ctx'=16,'head'=8] {'ctx'}, dimensions={0} | all-to-all | bytes 589824 | tf_op jit(solution)/shard_map/all_to_all | solution.py:389
  159.9 0.3 merge.1
  160.2 14.5 %all_to_all.33 = bf16[8,8,1024]{2,1,0:T(8,128)(2,1)S(1)} all-to-all(bf16[8,8,1024]{2,1,0:T(8,128)(2,1)S(1)} %bitcast.10), channel_id=1, replica_groups=mesh['ctx'=16,'head'=8] {'head'}, dimensions={0} | all-to-all | bytes 262144 | tf_op jit(solution)/shard_map/all_to_all | solution.py:398
  174.7 0.1 copy.10
  174.8 0.7 reshape.19

commit v4 on v3

--- a/solution.py
+++ b/solution.py
@@ -20,6 +20,7 @@
 TILE = 256
 ROWBLK = 256
 KEYBLK = 1024
+SUFFIX_ORDER = ((0, 0), (1, 0), (0, 1), (2, 0), (1, 1), (0, 2), (2, 1), (1, 2), (2, 2))
 
 f32 = jnp.float32
 bf16 = jnp.bfloat16
@@ -67,7 +68,7 @@
 
 def attend_kernel(
     scale, table_ref, home_ref, q_ref, pk_ref, pv_ref, sk_ref, sv_ref, out_ref, fresh_ref,
-    kbuf, vbuf, vturn, skbuf, svbuf, qrow, top, acc, total, qslot, oraw, lraw, oslot, lslot, ksem, vsem, ssem,
+    kbuf, vbuf, vturn, skbuf, svbuf, qrow, top, acc, total, qslot, oslot, lslot, ksem, vsem, ssem,
 ):
     req_rows = q_ref.shape[0]
     groups = q_ref.shape[1] // HD
@@ -84,10 +85,12 @@
             pltpu.make_async_copy(pv_ref.at[at], vbuf.at[at], vsem.at[i]),
         )
 
-    def suffix_copies(s):
+    def suffix_copies(i, n):
+        s = i * per_step + n
+        lanes = pl.ds(n * HD, HD)
         return (
-            pltpu.make_async_copy(sk_ref.at[s], skbuf.at[s], ssem.at[0, s]),
-            pltpu.make_async_copy(sv_ref.at[s], svbuf.at[s], ssem.at[1, s]),
+            pltpu.make_async_copy(sk_ref.at[s], skbuf.at[i, :, lanes], ssem.at[0, s]),
+            pltpu.make_async_copy(sv_ref.at[s], svbuf.at[i, :, lanes], ssem.at[1, s]),
         )
 
     for copy in prefix_copies(0):
@@ -144,8 +147,8 @@
         def score():
             q = blocks(lambda s: qslot[pl.ds(pl.multiple_of(s * slot_rows, slot_rows), slot_rows)])
             live = blocks(lambda s: position < lengths[s * TOKENS : s * TOKENS + 1])
-            keys = jnp.concatenate([skbuf[s] for s in slots], axis=1)
-            held["scores"] = jnp.where(live, dot_t(apart(q).astype(bf16), keys) * scale, NEG_BIG)
+            keys = skbuf[slots[0] // per_step]
+            held["scores"] = jnp.where(live, jnp.transpose(dot_t(keys, apart(q).astype(bf16))) * scale, NEG_BIG)
 
         def weigh():
             scores = held["scores"]
@@ -155,14 +158,19 @@
             held["high"], held["p"] = high, p.astype(bf16)
 
         def mix():
-            values = jnp.concatenate([svbuf[s] for s in slots], axis=1)
+            values = svbuf[slots[0] // per_step]
             wide = dot(held["p"], values)
             level = held["high"] + jnp.log(held["sum"]) * LOG2E
             for n, s in enumerate(slots):
                 at = slice(n * slot_rows, (n + 1) * slot_rows)
                 mixed = wide[at, n * HD : (n + 1) * HD]
-                oraw[s] = mixed / held["sum"][at]
-                lraw[s] = jnp.broadcast_to(level[at], mixed.shape)
+                mixed = mixed * (1.0 / held["sum"][at])
+                wide_level = jnp.broadcast_to(level[at], mixed.shape)
+                for g in range(groups):
+                    put_rows = slice(s * TOKENS, (s + 1) * TOKENS)
+                    lanes = slice(g * HD, (g + 1) * HD)
+                    oslot[put_rows, lanes] = mixed[g * TOKENS : (g + 1) * TOKENS]
+                    lslot[put_rows, lanes] = wide_level[g * TOKENS : (g + 1) * TOKENS]
 
         return [score, weigh, mix]
 
@@ -175,12 +183,12 @@
         for copy in prefix_copies(i + 1):
             copy.start()
         for n in range(per_step):
-            for copy in suffix_copies(i * per_step + n):
+            for copy in suffix_copies(i, n):
                 copy.start()
 
     def wait_suffix(i):
         for n in range(per_step):
-            for copy in suffix_copies(i * per_step + n):
+            for copy in suffix_copies(i, n):
                 copy.wait()
 
     def prefix_chunk(i):
@@ -250,23 +258,16 @@
     for i in range(chunks - 1):
         wait_suffix(i)
     staged = [suffix_stages([i * per_step + n for n in range(per_step)]) for i in range(chunks - 1)]
-    for m in range(3):
-        for stages in staged:
-            stages[m]()
     oslot[...] = jnp.zeros_like(oslot)
     lslot[...] = jnp.zeros_like(lslot)
-    for s in range(slot_count):
-        for g in range(groups):
-            put_rows = slice(s * TOKENS, (s + 1) * TOKENS)
-            lanes = slice(g * HD, (g + 1) * HD)
-            oslot[put_rows, lanes] = oraw[s, g * TOKENS : (g + 1) * TOKENS]
-            lslot[put_rows, lanes] = lraw[s, g * TOKENS : (g + 1) * TOKENS]
+    for pair, m in SUFFIX_ORDER:
+        staged[pair][m]()
     same_row = lax.broadcasted_iota(jnp.int32, (req_rows, req_rows), 0)
     same_col = lax.broadcasted_iota(jnp.int32, (req_rows, req_rows), 1)
     put_f = dot_t(jnp.where(same_row == same_col, 1.0, 0.0).astype(bf16), pick)
-    put = put_f.astype(bf16)
-    suffix_mix = sum(dot(put, piece) for piece in pieces(oslot[...]))
-    suffix_level = sum(dot(put, piece) for piece in pieces(lslot[...]))
+    put = jnp.concatenate([put_f] * 3, axis=1).astype(bf16)
+    suffix_mix = dot(put, jnp.concatenate(pieces(oslot[...]), axis=0))
+    suffix_level = dot(put, jnp.concatenate(pieces(lslot[...]), axis=0))
     has_suffix = jnp.sum(put_f, axis=1, keepdims=True) > 0.5
     lane = lax.broadcasted_iota(jnp.int32, (req_rows, HD), 1)
     levels = jnp.zeros((req_rows, HD), f32)
@@ -275,13 +276,13 @@
         lanes = slice(g * HD, (g + 1) * HD)
         level = top[0:1, at] + jnp.log(total[0:1, at]) * LOG2E
         level = jnp.transpose(jnp.broadcast_to(level, (HD, req_rows)))
-        prefix_mix = jnp.transpose(acc[:, at] / total[0:1, at])
+        prefix_mix = jnp.transpose(acc[:, at] * (1.0 / total[0:1, at]))
         other = jnp.where(has_suffix, suffix_level[:, lanes], NEG_BIG)
         high = jnp.maximum(level, other)
         mine = jnp.exp2(level - high)
         theirs = jnp.exp2(other - high)
         summed = mine + theirs
-        mixed = (prefix_mix * mine + suffix_mix[:, lanes] * theirs) / summed
+        mixed = (prefix_mix * mine + suffix_mix[:, lanes] * theirs) * (1.0 / summed)
         out_ref[:, lanes] = mixed.astype(bf16)
         level = high + jnp.log(summed) * LOG2E
         for j, piece in enumerate(pieces(level)):
@@ -297,6 +298,8 @@
     slot_count = suffix_k.shape[0]
     slot_rows = groups * TOKENS
     chunks = prefix_k.shape[0] // CHUNK
+    per_step = slot_count // (chunks - 1)
+    paired = (slot_count // per_step, suffix_k.shape[1], per_step * HD)
     vmem = pl.BlockSpec(memory_space=pltpu.VMEM)
     hbm = pl.BlockSpec(memory_space=pl.ANY)
     return pl.pallas_call(
@@ -311,15 +314,13 @@
             pltpu.VMEM(prefix_k.shape, bf16),
             pltpu.VMEM(prefix_v.shape, bf16),
             pltpu.VMEM((HD, CHUNK), bf16),
-            pltpu.VMEM(suffix_k.shape, bf16),
-            pltpu.VMEM(suffix_v.shape, bf16),
+            pltpu.VMEM(paired, bf16),
+            pltpu.VMEM(paired, bf16),
             pltpu.VMEM((rows, HD), bf16),
             pltpu.VMEM((8, rows), f32),
             pltpu.VMEM((HD, rows), f32),
             pltpu.VMEM((8, rows), f32),
             pltpu.VMEM((slot_count * slot_rows, HD), f32),
-            pltpu.VMEM((slot_count, slot_rows, HD), f32),
-            pltpu.VMEM((slot_count, slot_rows, HD), f32),
             pltpu.VMEM((PAD, width), f32),
             pltpu.VMEM((PAD, width), f32),
             pltpu.SemaphoreType.DMA((chunks,)),

time: 176 us -> 175 us (level)
  no operation moved by 1% of the time
where the time goes in v4:
time: 175 us; the launch traced here: 174 us
  blocking collectives  151 us (86%)
  Pallas kernels  22.6 us (13%)
    all_to_all x1, blocking collectives, on_device(): lax.all_to_all(parts, 'ctx', split_axis=0, concat_axis=0, tiled=True)  122 us
    pallas_call x1, Pallas kernels, attend(): pl.pallas_call(functools.partial(attend_kernel, HD ** (-0.5) * LOG2E), in...  21.5 us
    all_to_all x1, blocking collectives, on_device(): lax.all_to_all(finished, 'head', split_axis=0, concat_axis=0, tiled=True)  14.5 us
    all_to_all x1, blocking collectives, on_device(): lax.all_to_all(sent, 'ctx', split_axis=0, concat_axis=0, tiled=True)  14.4 us

profile of v4, /device:TPU:0, one launch (start us, length us, event | category | flops | bytes accessed | tf_op | source)
XLA Modules:
  0.0 174.4 jit_solution(2755168738655270454)
XLA Ops:
  0.0 0.8 spread.1
  0.8 14.4 %all_to_all.31 = bf16[16,8,1024]{2,1,0:T(8,128)(2,1)S(1)} all-to-all(bf16[16,8,1024]{2,1,0:T(8,128)(2,1)S(1)} %bitcast.12), channel_id=1, replica_groups=mesh['ctx'=16,'head'=8] {'ctx'}, dimensions={0} | all-to-all | bytes 524288 | tf_op jit(solution)/shard_map/all_to_all | solution.py:387
  15.2 21.5 %attend.1 = (bf16[128,1152]{1,0:T(8,128)(2,1)S(1)}, f32[8,2048]{1,0:T(8,128)S(1)}) custom-call(s32[2,64]{1,0:T(2,128)S(1)} %get-tuple-element.10.table_ref, f32[8,1280]{1,0:T(8,128)S(1)} %get-tuple-element.11.home_ref, bf16[128,1024]{1,0:T(8,128)(2,1)S(1)} %bitcast.9, bf16[16384,128]{1,0:T(8,128)(2,1)} %pk_ref.1, bf16[16384,128]{1,0:T(8,128)(2,1)} %pv_ref.1, ...), custom_call_target="tpu_custom_call" | custom-call | tf_op jit(solution)/shard_map/attend/pallas_call | solution.py:305
  36.7 122.1 %all_to_all.32 = bf16[16,8,1152]{2,1,0:T(8,128)(2,1)S(1)} all-to-all(bf16[16,8,1152]{2,1,0:T(8,128)(2,1)S(1)} %bitcast.11), channel_id=1, replica_groups=mesh['ctx'=16,'head'=8] {'ctx'}, dimensions={0} | all-to-all | bytes 589824 | tf_op jit(solution)/shard_map/all_to_all | solution.py:390
  158.8 0.3 merge.1
  159.1 14.5 %all_to_all.33 = bf16[8,8,1024]{2,1,0:T(8,128)(2,1)S(1)} all-to-all(bf16[8,8,1024]{2,1,0:T(8,128)(2,1)S(1)} %bitcast.10), channel_id=1, replica_groups=mesh['ctx'=16,'head'=8] {'head'}, dimensions={0} | all-to-all | bytes 262144 | tf_op jit(solution)/shard_map/all_to_all | solution.py:399
  173.6 0.1 copy.10
  173.7 0.7 reshape.19

commit v5 on v4

--- a/solution.py
+++ b/solution.py
@@ -68,7 +68,7 @@
 
 def attend_kernel(
     scale, table_ref, home_ref, q_ref, pk_ref, pv_ref, sk_ref, sv_ref, out_ref, fresh_ref,
-    kbuf, vbuf, vturn, skbuf, svbuf, qrow, top, acc, total, qslot, oslot, lslot, ksem, vsem, ssem,
+    kfirst, kbuf, vbuf, vturn, skbuf, svbuf, qrow, top, acc, total, qslot, oslot, lslot, fsem, ksem, vsem, ssem,
 ):
     req_rows = q_ref.shape[0]
     groups = q_ref.shape[1] // HD
@@ -93,6 +93,8 @@
             pltpu.make_async_copy(sv_ref.at[s], svbuf.at[i, :, lanes], ssem.at[1, s]),
         )
 
+    first_keys = pltpu.make_async_copy(pk_ref.at[pl.ds(0, TILE)], kfirst, fsem)
+    first_keys.start()
     for copy in prefix_copies(0):
         copy.start()
 
@@ -176,7 +178,7 @@
 
     def first_top():
         for r in range(0, rows, ROWBLK):
-            high = jnp.max(dot_t(kbuf[0:TILE], qrow[r : r + ROWBLK]), axis=0, keepdims=True) * scale
+            high = jnp.max(dot_t(kfirst[...], qrow[r : r + ROWBLK]), axis=0, keepdims=True) * scale
             top[:, r : r + ROWBLK] = jnp.broadcast_to(high, (8, ROWBLK))
 
     def start_next(i):
@@ -219,11 +221,12 @@
         keys_copy, values_copy = prefix_copies(i)
         keys_copy.wait()
         pl.when(i + 1 < chunks)(lambda: start_next(i))
-        pl.when(i == 0)(first_top)
         values_copy.wait()
         prefix_chunk(i)
         return 0
 
+    first_keys.wait()
+    first_top()
     lax.fori_loop(0, chunks, step, 0)
     summed = jnp.sum(total[...], axis=0, keepdims=True)
     total[...] = jnp.broadcast_to(summed, total.shape)
@@ -311,6 +314,7 @@
             pltpu.VMEM((home.shape[0], 2 * width), f32),
         ],
         scratch_shapes=[
+            pltpu.VMEM((TILE, HD), bf16),
             pltpu.VMEM(prefix_k.shape, bf16),
             pltpu.VMEM(prefix_v.shape, bf16),
             pltpu.VMEM((HD, CHUNK), bf16),
@@ -323,6 +327,7 @@
             pltpu.VMEM((slot_count * slot_rows, HD), f32),
             pltpu.VMEM((PAD, width), f32),
             pltpu.VMEM((PAD, width), f32),
+            pltpu.SemaphoreType.DMA,
             pltpu.SemaphoreType.DMA((chunks,)),
             pltpu.SemaphoreType.DMA((chunks,)),
             pltpu.SemaphoreType.DMA((2, slot_count)),

time: 175 us -> 175 us (level)
  no operation moved by 1% of the time
where the time goes in v5:
time: 175 us
  blocking collectives  152 us (87%)
  Pallas kernels  22.3 us (13%)
    all_to_all x1, blocking collectives, on_device(): lax.all_to_all(parts, 'ctx', split_axis=0, concat_axis=0, tiled=True)  123 us
    pallas_call x1, Pallas kernels, attend(): pl.pallas_call(functools.partial(attend_kernel, HD ** (-0.5) * LOG2E), in...  21.2 us
    all_to_all x1, blocking collectives, on_device(): lax.all_to_all(finished, 'head', split_axis=0, concat_axis=0, tiled=True)  14.5 us
    all_to_all x1, blocking collectives, on_device(): lax.all_to_all(sent, 'ctx', split_axis=0, concat_axis=0, tiled=True)  14.4 us

profile of v5, /device:TPU:0, one launch (start us, length us, event | category | flops | bytes accessed | tf_op | source)
XLA Modules:
  0.0 174.7 jit_solution(9478624588827857744)
XLA Ops:
  0.0 0.8 spread.1
  0.8 14.4 %all_to_all.31 = bf16[16,8,1024]{2,1,0:T(8,128)(2,1)S(1)} all-to-all(bf16[16,8,1024]{2,1,0:T(8,128)(2,1)S(1)} %bitcast.12), channel_id=1, replica_groups=mesh['ctx'=16,'head'=8] {'ctx'}, dimensions={0} | all-to-all | bytes 524288 | tf_op jit(solution)/shard_map/all_to_all | solution.py:392
  15.2 21.2 %attend.1 = (bf16[128,1152]{1,0:T(8,128)(2,1)S(1)}, f32[8,2048]{1,0:T(8,128)S(1)}) custom-call(s32[2,64]{1,0:T(2,128)S(1)} %get-tuple-element.10.table_ref, f32[8,1280]{1,0:T(8,128)S(1)} %get-tuple-element.11.home_ref, bf16[128,1024]{1,0:T(8,128)(2,1)S(1)} %bitcast.9, bf16[16384,128]{1,0:T(8,128)(2,1)} %pk_ref.1, bf16[16384,128]{1,0:T(8,128)(2,1)} %pv_ref.1, ...), custom_call_target="tpu_custom_call" | custom-call | tf_op jit(solution)/shard_map/attend/pallas_call | solution.py:308
  36.4 122.6 %all_to_all.32 = bf16[16,8,1152]{2,1,0:T(8,128)(2,1)S(1)} all-to-all(bf16[16,8,1152]{2,1,0:T(8,128)(2,1)S(1)} %bitcast.11), channel_id=1, replica_groups=mesh['ctx'=16,'head'=8] {'ctx'}, dimensions={0} | all-to-all | bytes 589824 | tf_op jit(solution)/shard_map/all_to_all | solution.py:395
  159.0 0.3 merge.1
  159.3 14.5 %all_to_all.33 = bf16[8,8,1024]{2,1,0:T(8,128)(2,1)S(1)} all-to-all(bf16[8,8,1024]{2,1,0:T(8,128)(2,1)S(1)} %bitcast.10), channel_id=1, replica_groups=mesh['ctx'=16,'head'=8] {'head'}, dimensions={0} | all-to-all | bytes 262144 | tf_op jit(solution)/shard_map/all_to_all | solution.py:404
  173.9 0.1 copy.10
  173.9 0.7 reshape.19
